TPU v7x, 32 devices: a whole 2x2x4 slice. The times are simulated.
32 devices in a mesh: dp: 8 (over y, x, core), mp: 4 (over z).
Axes of the slice: x: 2, y: 2, z: 4, core: 2. Of those that a mesh axis runs over, the one named last changes fastest.
Arguments:
- inputs: bfloat16 [16, 16, 4096], P('dp')
- denoiser: int32 [16], P('dp'), may hold values from 0 to 2
- span_mask: int32 [16, 16], P('dp'), may hold values 0 or 1
- lengths: int32 [16], P('dp'), may hold values from 4 to 16
- move_plan: int32 [16], P('dp'), may hold values from -1 to 1, as said below
- mode_table: bfloat16 [3, 4096], replicated, may hold values from -3 to 3
- sentinel: bfloat16 [4096], replicated, may hold values from -6 to 6
- w_query: bfloat16 [4096, 1024], P(None, 'mp')
- w_key: bfloat16 [4096, 1024], P(None, 'mp')
- w_value: bfloat16 [4096, 1024], P(None, 'mp'), may hold values from -0.09375 to 0.09375
- cotangent: bfloat16 [32, 16, 1024], P('dp', None, 'mp'), may hold values from -6 to 6
Outputs:
- context: bfloat16 [32, 16, 1024], P('dp', None, 'mp')
- input_grad: bfloat16 [16, 16, 4096], P('dp', 'mp')
Inputs may be any that keep to these rules, and one draw needn't show every extreme that they name: `move_plan`: every row stays (0) or moves to the next (1) or previous (-1) data group along dp, cyclically. A data group sends at most one row to each of its two neighbours, and in every draw some data group receives a row from both neighbours.
All inputs are finite; a program needn't handle non-finite values. No bound on the sum of `span_mask` on one device may be relied on, other than what follows from the above.
Results may differ from a plain program's by a relative error of at most 0.02.
The roundings to bfloat16 on the way count: a program that leaves them out, or rounds other values in their place, can miss the bound.
Values may be sent and summed in bfloat16 or wider, within the bound.
A program may use at most 64 MiB of HBM per device.

v0:
```python
import math

import jax
import jax.numpy as jnp
from jax import lax
from jax.sharding import PartitionSpec as P


def shifted(array, axis, by):
    devices = lax.axis_size(axis)
    return lax.ppermute(array, axis, [(i, (i + by) % devices) for i in range(devices)])


def attend(slot_rows, slot_len, cotangent, w_query, w_key, w_value):
    slot_count, length, model_width = slot_rows.shape
    head_size = w_query.shape[1]
    flat_rows = slot_rows.astype(jnp.float32).reshape(slot_count * length, model_width)
    inv_rms = lax.rsqrt(jnp.mean(flat_rows * flat_rows, axis=1, keepdims=True) + 1e-06)
    normed = flat_rows * inv_rms
    normed_b = normed.astype(jnp.bfloat16)

    def project(weight):
        result = jnp.dot(normed_b, weight, preferred_element_type=jnp.float32)
        return result.astype(jnp.bfloat16).reshape(slot_count, length, head_size)

    query_rows = project(w_query)
    key_rows = project(w_key)
    value_rows = project(w_value)
    positions = jnp.arange(length, dtype=jnp.int32)
    key_ok = positions[None, None, :] < jnp.maximum(slot_len, 1)[:, None, None]
    query_ok = positions[None, :, None] < slot_len[:, None, None]
    factor = 1.0 / math.sqrt(head_size)
    scores = (
        jnp.einsum("sqd,skd->sqk", query_rows, key_rows, preferred_element_type=jnp.float32)
        * factor
    )
    scores = jnp.where(key_ok, scores, -jnp.inf)
    row_max = jnp.max(scores, axis=2, keepdims=True)
    exp_scores = jnp.exp(scores - row_max)
    soft = exp_scores / jnp.sum(exp_scores, axis=2, keepdims=True)
    soft_b = soft.astype(jnp.bfloat16)
    context = jnp.einsum("sqk,skd->sqd", soft_b, value_rows, preferred_element_type=jnp.float32)
    context = (context * query_ok.astype(jnp.float32)).astype(jnp.bfloat16)
    grad_out = jnp.where(query_ok, cotangent, jnp.zeros_like(cotangent))
    grad_value = jnp.einsum(
        "sqk,sqd->skd", soft_b, grad_out, preferred_element_type=jnp.float32
    ).astype(jnp.bfloat16)
    grad_soft = jnp.einsum("sqd,skd->sqk", grad_out, value_rows, preferred_element_type=jnp.float32)
    row_inner = jnp.sum(soft * grad_soft, axis=2, keepdims=True)
    grad_scores = (soft * (grad_soft - row_inner) * factor).astype(jnp.bfloat16)
    grad_query = jnp.einsum(
        "sqk,skd->sqd", grad_scores, key_rows, preferred_element_type=jnp.float32
    ).astype(jnp.bfloat16)
    grad_key = jnp.einsum(
        "sqk,sqd->skd", grad_scores, query_rows, preferred_element_type=jnp.float32
    ).astype(jnp.bfloat16)

    def project_back(gradient, weight):
        flat_grad = gradient.reshape(slot_count * length, head_size)
        return lax.dot_general(
            flat_grad, weight, (((1,), (1,)), ((), ())), preferred_element_type=jnp.float32
        )

    head_grad = (
        project_back(grad_query, w_query)
        + project_back(grad_key, w_key)
        + project_back(grad_value, w_value)
    )
    inner_norm = jnp.mean(head_grad * normed, axis=1, keepdims=True)
    head_part = ((head_grad - normed * inner_norm) * inv_rms).astype(jnp.bfloat16)
    return (context, head_part.reshape(slot_count, length, model_width))


def shards(
    inputs,
    denoiser,
    span_mask,
    lengths,
    move_plan,
    mode_table,
    sentinel,
    w_query,
    w_key,
    w_value,
    cotangent,
):
    rows_dev, length, model_width = inputs.shape
    seg_rows = length // lax.axis_size("mp")
    offset_start = lax.axis_index("mp") * seg_rows
    mode_count = mode_table.shape[0]
    picked = (denoiser[:, None] == jnp.arange(mode_count, dtype=jnp.int32)[None, :]).astype(
        jnp.float32
    )
    mode_rows = jnp.sum(picked[:, :, None] * mode_table.astype(jnp.float32)[None, :, :], axis=1)
    span_flag = (span_mask == 1)[:, :, None]
    shaped = jnp.where(
        span_flag,
        sentinel.astype(jnp.float32)[None, None, :],
        inputs.astype(jnp.float32) + mode_rows[:, None, :],
    ).astype(jnp.bfloat16)
    goes_right = move_plan == 1
    goes_left = move_plan == -1
    stays = move_plan == 0

    def outgoing(flags):
        chosen = jnp.argmax(flags.astype(jnp.int32))
        picked_row = jnp.where(jnp.any(flags), shaped[chosen], jnp.zeros_like(shaped[0]))
        picked_len = jnp.sum(jnp.where(flags, lengths, 0)).reshape(1)
        return (picked_row, picked_len)

    right_rows, right_len = outgoing(goes_right)
    left_rows, left_len = outgoing(goes_left)

    def carry_whole(payload, offset):
        return shifted((payload[0], payload[1]), "dp", offset)

    from_left_rows, from_left_len = carry_whole((right_rows, right_len), 1)
    from_right_rows, from_right_len = carry_whole((left_rows, left_len), -1)
    arrived = jnp.stack([from_left_rows, from_right_rows])
    slot_rows = jnp.concatenate([shaped, arrived], axis=0)
    slot_len = jnp.concatenate(
        [jnp.where(stays, lengths, 0), from_left_len, from_right_len]
    ).astype(jnp.int32)
    context, head_part = attend(slot_rows, slot_len, cotangent, w_query, w_key, w_value)
    span_piece = lax.dynamic_slice_in_dim(span_mask, offset_start, seg_rows, 1)

    def carry_part(payload, offset):
        return shifted(payload, "dp", offset)

    back_right = carry_part(head_part[rows_dev], -1)
    back_left = carry_part(head_part[rows_dev + 1], 1)
    own_rows = head_part[:rows_dev]
    merged = jnp.where(
        stays[:, None, None],
        own_rows,
        jnp.where(
            goes_right[:, None, None],
            back_right[None, :, :],
            jnp.where(goes_left[:, None, None], back_left[None, :, :], jnp.zeros_like(own_rows)),
        ),
    )
    summed = lax.psum_scatter(
        merged.astype(jnp.float32).astype(jnp.bfloat16), "mp", scatter_dimension=1, tiled=True
    )
    input_grad = jnp.where((span_piece == 1)[:, :, None], jnp.zeros_like(summed), summed)
    return (context, input_grad)


def solution(mesh):
    return jax.shard_map(
        shards,
        mesh=mesh,
        in_specs=(
            P("dp", None, None),
            P("dp"),
            P("dp", None),
            P("dp"),
            P("dp"),
            P(),
            P(),
            P(None, "mp"),
            P(None, "mp"),
            P(None, "mp"),
            P("dp", None, "mp"),
        ),
        out_specs=(P("dp", None, "mp"), P("dp", "mp", None)),
        check_vma=False,
    )
```

profile of v0, /device:TPU:0, one launch (start us, length us, event | category | flops | bytes accessed | tf_op | source)
XLA Modules:
  0.0 92.9 jit_solution(600119216208941319)
XLA Ops:
  7.2 0.0 copy-start
  7.2 0.0 all-reduce.3.cloned.1.call-start
  7.2 1.4 %iota_reduce_fusion.1 = (s32[]{:T(128)}, s32[]{:T(128)}) fusion(s32[2]{0:T(128)} %param.15), kind=kLoop, calls=%fused_computation.52 | loop fusion | flops 11 | bytes 16 | tf_op jit(solution)/shard_map/shards.<locals>.outgoing/reduce | solution.py:106
  8.7 1.4 %fusion.30 = (pred[]{:T(512)}, pred[]{:T(512)}, pred[2]{0:T(512)(128)(4,1)S(1)}, pred[2]{0:T(512)(128)(4,1)S(1)}, pred[2]{0:T(512)(128)(4,1)S(1)}) fusion(s32[2]{0:T(128)} %param.15), kind=kLoop, calls=%fused_computation.69 | loop fusion | flops 8 | bytes 16 | tf_op jit(solution)/shard_map/reduce_or | solution.py:107
  10.0 1.3 %iota_reduce_fusion = (s32[]{:T(128)}, s32[]{:T(128)}) fusion(s32[2]{0:T(128)} %param.15), kind=kLoop, calls=%fused_computation.51 | loop fusion | flops 11 | bytes 16 | tf_op jit(solution)/shard_map/shards.<locals>.outgoing/reduce | solution.py:106
  13.9 0.8 convert_element_type.81
  14.7 0.7 fusion.22
  15.4 0.7 broadcast_compare_fusion
  16.1 0.1 multiply_reduce_fusion.2
  17.5 1.1 %select_convert_fusion = bf16[2,16,4096]{2,1,0:T(8,128)(2,1)S(1)} fusion(bf16[2,16,4096]{2,1,0:T(8,128)(2,1)} %param.11, f32[2,4096]{1,0:T(2,128)S(1)} %multiply_reduce_fusion.2, bf16[4096]{0:T(1024)(128)(2,1)} %param.17, pred[2,16]{1,0:T(4,128)(4,1)S(1)} %broadcast_compare_fusion), kind=kLoop, calls=%fused_computation.26 | loop fusion | flops 393216 | bytes 565280 | tf_op jit(solution)/shard_map/convert_element_type | solution.py:100
  18.5 1.4 %select_bitcast_fusion.1 = (bf16[16,4096]{1,0:T(8,128)(2,1)S(1)}, bf16[16,4096]{1,0:T(8,128)(2,1)S(1)}) fusion(bf16[2,16,4096]{2,1,0:T(8,128)(2,1)S(1)} %select_convert_fusion, s32[]{:T(128)S(6)} %select_n.77, pred[]{:T(512)} %get-tuple-element.8, s32[]{:T(128)S(6)} %select_n.81, pred[]{:T(512)} %get-tuple-element.9), kind=kLoop, calls=%fused_computation.29 | loop fusion | flops 131072 | bytes 524298 | tf_op jit(solution)/shard_map/jit(_where)/select_n | solution.py:107
  19.9 3.4 %collective-permute-start.3 = (bf16[16,4096]{1,0:T(8,128)(2,1)S(1)}, bf16[16,4096]{1,0:T(8,128)(2,1)S(1)}, u32[]{:S(2)}, u32[]{:S(2)}) collective-permute-start(bf16[16,4096]{1,0:T(8,128)(2,1)S(1)} %get-tuple-element.15), channel_id=1, source_target_pairs={{0,28},{4,0},{8,4},{12,8},{16,12},{20,16},{24,20},{28,24},{1,29},{... | collective-permute-start | bytes 393224 | tf_op jit(solution)/shard_map/ppermute | solution.py:11
  23.3 0.0 collective-permute-start.2
  23.3 1.3 %select_reduce_fusion.1 = (s32[]{:T(128)}, s32[]{:T(128)}, s32[2]{0:T(128)S(1)}) fusion(s32[2]{0:T(128)} %param.14, s32[2]{0:T(128)} %param.15), kind=kLoop, calls=%fused_computation.55 | loop fusion | flops 14 | bytes 32 | tf_op jit(solution)/shard_map/reduce_sum | solution.py:108
  24.6 2.6 %collective-permute-start.1 = (s32[1]{0:T(128)}, s32[1]{0:T(128)}, u32[]{:S(2)}, u32[]{:S(2)}) collective-permute-start(s32[1]{0:T(128)} %bitcast.1), channel_id=1, source_target_pairs={{0,28},{4,0},{8,4},{12,8},{16,12},{20,16},{24,20},{28,24},{1,29},{... | collective-permute-start | bytes 20 | tf_op jit(solution)/shard_map/ppermute | solution.py:11
  27.2 0.0 collective-permute-start
  27.2 1.4 %collective-permute-done.1 = s32[1]{0:T(128)} collective-permute-done((s32[1]{0:T(128)}, s32[1]{0:T(128)}, u32[]{:S(2)}, u32[]{:S(2)}) %collective-permute-start.1) | collective-permute-done | bytes 36 | tf_op jit(solution)/shard_map/ppermute | solution.py:11
  28.7 2.7 %collective-permute-done = s32[1]{0:T(128)} collective-permute-done((s32[1]{0:T(128)}, s32[1]{0:T(128)}, u32[]{:S(2)}, u32[]{:S(2)}) %collective-permute-start) | collective-permute-done | bytes 36 | tf_op jit(solution)/shard_map/ppermute | solution.py:11
  31.3 1.3 %broadcast_maximum_fusion = (s32[4]{0:T(128)S(1)}, s32[4]{0:T(128)S(1)}) fusion(s32[1]{0:T(128)} %collective-permute-done.1, s32[1]{0:T(128)} %collective-permute-done, s32[2]{0:T(128)S(1)} %get-tuple-element.16), kind=kLoop, calls=%fused_computation.59 | loop fusion | flops 12 | bytes 48 | tf_op jit(solution)/shard_map/max | solution.py:30
  32.7 0.1 iota_compare_fusion
  32.7 0.0 collective-permute-done.3
  32.7 0.0 collective-permute-done.2
  32.8 0.2 multiply_reduce_fusion.1
  32.9 0.1 rsqrt.12
  33.0 0.0 copy-start.1
  33.0 0.2 fusion.10
  33.2 0.0 copy-done
  33.2 0.0 copy-start.2
  33.2 0.5 convolution_convert_fusion.3
  33.7 0.9 %copy-done.1 = bf16[4096,256]{1,0:T(8,128)(2,1)S(1)} copy-done((bf16[4096,256]{1,0:T(8,128)(2,1)S(1)}, bf16[4096,256]{1,0:T(8,128)(2,1)}, u32[]{:S(2)}) %copy-start.1) | copy-done | bytes 2097176
  34.6 0.0 copy-start.5
  34.6 0.5 convolution_convert_fusion.5
  35.1 0.2 copy-done.2
  35.3 0.5 convolution_convert_fusion.4
  35.8 0.1 fusion.8
  35.9 0.1 fusion.33
  36.0 0.0 copy-done.5
  36.0 0.2 fusion.15
  36.2 0.2 convolution_convert_fusion.2
  36.5 0.1 convolution_convert_fusion.1
  36.6 0.2 convolution_convert_fusion
  36.8 0.0 copy-start.3
  36.8 2.5 %fusion.34 = f32[64,4096]{1,0:T(8,128)S(1)} fusion(bf16[64,256]{1,0:T(8,128)(2,1)S(1)} %bitcast.60, bf16[4096,256]{1,0:T(8,128)(2,1)} %param.18), kind=kOutput, calls=%fused_computation.73 | convolution fusion | flops 134217728 | bytes 3178496 | tf_op jit(solution)/shard_map/dot_general | solution.py:60
  39.3 0.0 copy-done.3
  39.3 0.8 convolution_add_fusion.1
  40.1 0.9 multiply_reduce_fusion
  40.9 0.0 copy-start.4
  41.0 0.0 copy-start.6
  41.0 0.3 multiply_convert_fusion
  41.3 0.1 collective-permute-start.5
  41.3 2.6 %collective-permute-start.4 = (bf16[16,4096]{1,0:T(8,128)(2,1)S(1)}, bf16[16,4096]{1,0:T(8,128)(2,1)S(1)}, u32[]{:S(2)}, u32[]{:S(2)}) collective-permute-start(bf16[16,4096]{1,0:T(8,128)(2,1)S(1)} %get-tuple-element.12), channel_id=1, source_target_pairs={{0,28},{4,0},{8,4},{12,8},{16,12},{20,16},{24,20},{28,24},{1,29},{... | collective-permute-start | bytes 393224 | tf_op jit(solution)/shard_map/ppermute | solution.py:11
  44.0 2.6 %collective-permute-done.5 = bf16[16,4096]{1,0:T(8,128)(2,1)S(1)} collective-permute-done((bf16[16,4096]{1,0:T(8,128)(2,1)S(1)}, bf16[16,4096]{1,0:T(8,128)(2,1)S(1)}, u32[]{:S(2)}, u32[]{:S(2)}) %collective-permute-start.5) | collective-permute-done | bytes 131104 | tf_op jit(solution)/shard_map/ppermute | solution.py:11
  46.6 0.0 collective-permute-done.4
  46.6 0.8 select_select_fusion
  47.4 0.0 all-reduce.3.cloned.1.call-update
  47.5 0.0 copy-done.4
  47.5 0.1 dynamic-slice_compare_fusion
  47.5 0.0 copy-done.6
  47.5 0.6 dynamic-slice
  48.8 0.8 fusion.2
  49.6 34.8 %all-reduce.3.cloned.1.call-done = bf16[2,16,4096]{2,1,0:T(8,128)(2,1)} async-done(((bf16[2,16,4096]{2,1,0:T(8,128)(2,1)}), bf16[2,16,4096]{2,1,0:T(8,128)(2,1)}) %all-reduce.3.cloned.1.call-update) | async-done | bytes 262160
  84.4 1.6 %dynamic-slice_select_fusion = bf16[2,4,4096]{2,1,0:T(4,128)(2,1)} fusion(bf16[2,16,4096]{2,1,0:T(8,128)(2,1)} %all-reduce.3.cloned.1.call-done, u32[]{:T(128)S(6)} %multiply.14, pred[2,4]{1,0:T(4,128)(4,1)S(1)} %dynamic-slice_compare_fusion), kind=kLoop, calls=%fused_computation.31 | loop fusion | flops 32768 | bytes 131084 | tf_op jit(solution)/shard_map/jit(_where)/select_n | solution.py:145
  (4 shorter events, 0.1 us)
Async XLA Ops:
  7.2 26.1 %copy-start = (bf16[4096,256]{1,0:T(8,128)(2,1)S(1)}, bf16[4096,256]{1,0:T(8,128)(2,1)}, u32[]{:S(2)}) copy-start(bf16[4096,256]{1,0:T(8,128)(2,1)} %param.20) | copy-start | bytes 6291460
  7.2 77.2 %all-reduce.3.cloned.1.call-start = ((), (), s32[]{:S(2)}) async-start(), calls=%async_computation | async-start | bytes 524288
  19.9 12.9 %collective-permute-start.3 = (bf16[16,4096]{1,0:T(8,128)(2,1)S(1)}, bf16[16,4096]{1,0:T(8,128)(2,1)S(1)}, u32[]{:S(2)}, u32[]{:S(2)}) collective-permute-start(bf16[16,4096]{1,0:T(8,128)(2,1)S(1)} %get-tuple-element.15), channel_id=1, source_target_pairs={{0,28},{4,0},{8,4},{12,8},{16,12},{20,16},{24,20},{28,24},{1,29},{... | collective-permute-start | bytes 393224 | tf_op jit(solution)/shard_map/ppermute | solution.py:11
  23.3 9.5 %collective-permute-start.2 = (bf16[16,4096]{1,0:T(8,128)(2,1)S(1)}, bf16[16,4096]{1,0:T(8,128)(2,1)S(1)}, u32[]{:S(2)}, u32[]{:S(2)}) collective-permute-start(bf16[16,4096]{1,0:T(8,128)(2,1)S(1)} %get-tuple-element.14), channel_id=1, source_target_pairs={{0,4},{4,8},{8,12},{12,16},{16,20},{20,24},{24,28},{28,0},{1,5},{5... | collective-permute-start | bytes 393224 | tf_op jit(solution)/shard_map/ppermute | solution.py:11
  24.6 4.1 %collective-permute-start.1 = (s32[1]{0:T(128)}, s32[1]{0:T(128)}, u32[]{:S(2)}, u32[]{:S(2)}) collective-permute-start(s32[1]{0:T(128)} %bitcast.1), channel_id=1, source_target_pairs={{0,28},{4,0},{8,4},{12,8},{16,12},{20,16},{24,20},{28,24},{1,29},{... | collective-permute-start | bytes 20 | tf_op jit(solution)/shard_map/ppermute | solution.py:11
  27.2 4.1 %collective-permute-start = (s32[1]{0:T(128)}, s32[1]{0:T(128)}, u32[]{:S(2)}, u32[]{:S(2)}) collective-permute-start(s32[1]{0:T(128)} %bitcast), channel_id=1, source_target_pairs={{0,4},{4,8},{8,12},{12,16},{16,20},{20,24},{24,28},{28,0},{1,5},{5... | collective-permute-start | bytes 20 | tf_op jit(solution)/shard_map/ppermute | solution.py:11
  33.0 1.6 %copy-start.1 = (bf16[4096,256]{1,0:T(8,128)(2,1)S(1)}, bf16[4096,256]{1,0:T(8,128)(2,1)}, u32[]{:S(2)}) copy-start(bf16[4096,256]{1,0:T(8,128)(2,1)} %param.18) | copy-start | bytes 6291460
  33.2 2.1 %copy-start.2 = (bf16[4096,256]{1,0:T(8,128)(2,1)S(1)}, bf16[4096,256]{1,0:T(8,128)(2,1)}, u32[]{:S(2)}) copy-start(bf16[4096,256]{1,0:T(8,128)(2,1)} %param.19) | copy-start | bytes 6291460
  34.6 1.4 %copy-start.5 = (bf16[4,16,256]{2,1,0:T(8,128)(2,1)S(1)}, bf16[4,16,256]{2,1,0:T(8,128)(2,1)}, u32[]{:S(2)}) copy-start(bf16[4,16,256]{2,1,0:T(8,128)(2,1)} %param.21) | copy-start | bytes 98308
  36.8 2.5 %copy-start.3 = (bf16[4096,256]{1,0:T(8,128)(2,1)S(1)}, bf16[4096,256]{1,0:T(8,128)(2,1)}, u32[]{:S(2)}) copy-start(bf16[4096,256]{1,0:T(8,128)(2,1)} %param.19) | copy-start | bytes 6291460
  40.9 6.5 %copy-start.4 = (s32[2,16]{1,0:T(2,128)S(1)}, s32[2,16]{1,0:T(2,128)}, u32[]{:S(2)}) copy-start(s32[2,16]{1,0:T(2,128)} %param.13) | copy-start | bytes 388
  41.0 6.6 %copy-start.6 = (u32[32]{0:T(128)S(1)}, u32[32]{0:T(128)}, u32[]{:S(2)}) copy-start(u32[32]{0:T(128)} %constant.54) | copy-start | bytes 388
  41.3 5.3 %collective-permute-start.5 = (bf16[16,4096]{1,0:T(8,128)(2,1)S(1)}, bf16[16,4096]{1,0:T(8,128)(2,1)S(1)}, u32[]{:S(2)}, u32[]{:S(2)}) collective-permute-start(bf16[16,4096]{1,0:T(8,128)(2,1)S(1)} %get-tuple-element.13), channel_id=1, source_target_pairs={{0,4},{4,8},{8,12},{12,16},{16,20},{20,24},{24,28},{28,0},{1,5},{5... | collective-permute-start | bytes 393224 | tf_op jit(solution)/shard_map/ppermute | solution.py:11
  41.3 5.3 %collective-permute-start.4 = (bf16[16,4096]{1,0:T(8,128)(2,1)S(1)}, bf16[16,4096]{1,0:T(8,128)(2,1)S(1)}, u32[]{:S(2)}, u32[]{:S(2)}) collective-permute-start(bf16[16,4096]{1,0:T(8,128)(2,1)S(1)} %get-tuple-element.12), channel_id=1, source_target_pairs={{0,28},{4,0},{8,4},{12,8},{16,12},{20,16},{24,20},{28,24},{1,29},{... | collective-permute-start | bytes 393224 | tf_op jit(solution)/shard_map/ppermute | solution.py:11
Sparse Core Ops, SparseCore 0:
  47.6 36.7 all-reduce.2
where the time goes:
time: 93.3 us; the launch traced here: 92.9 us
  waiting for transfers between devices  41.5 us (44%)
  between operations  18.7 us (20%)
  other arithmetic  14.8 us (16%)
  starting transfers between devices  8.76 us (9%)
  matrix products  7.2 us (8%)
  local copies, waits for them, and re-layouts  1.89 us (2%)
    unnamed x2, waiting for transfers between devices  34.8 us
    ppermute x6, starting transfers between devices, shifted(): lax.ppermute(array, axis, [(i, (i + by) % devices) for i in range(devices)])  8.72 us
    ppermute x6, waiting for transfers between devices, shifted(): lax.ppermute(array, axis, [(i, (i + by) % devices) for i in range(devices)])  6.73 us
    dot_general x3, matrix products, project_back(): lax.dot_general(flat_grad, weight, (((1,), (1,)), ((), ())), preferred_el...  4.11 us
    another operation x2, other arithmetic, outgoing(): chosen = jnp.argmax(flags.astype(jnp.int32))  2.78 us
  transfers between devices with their start and end apart: 7, of which 4 were waited for; matrix products, arithmetic and copies ran while one was open for 5% of the time, Pallas kernels for 0%

commit v1 on v0

v1 whole, which is shorter than its diff:
```python
import functools
import math

import jax
import jax.numpy as jnp
from jax import lax
from jax.experimental import pallas as pl
from jax.experimental.pallas import tpu as pltpu
from jax.sharding import PartitionSpec as P

MESH = pl.DeviceIdType.MESH
F32 = jnp.float32
BF16 = jnp.bfloat16
NT = (((1,), (1,)), ((), ()))
TN = (((0,), (0,)), ((), ()))
NN = (((1,), (0,)), ((), ()))

FORWARD_CHUNKS = 4
BACK_CHUNKS = 4
NORM_CHUNKS = 8


def matmul(a, b, dims=NN):
    return lax.dot_general(a, b, dims, preferred_element_type=F32)


def kernel(
    dp_count,
    mp_count,
    denoiser_ref,
    lengths_ref,
    move_ref,
    span_ref,
    table_ref,
    sentinel_ref,
    inputs_hbm,
    cot_hbm,
    wq_hbm,
    wk_hbm,
    wv_hbm,
    context_ref,
    grad_ref,
    inputs_ref,
    cot_ref,
    weights,
    normed_ref,
    normed_b_ref,
    cot_recv,
    ctx_send,
    part_send,
    part_recv,
    in_sem,
    w_sem,
    cot_send_sem,
    cot_recv_sem,
    ctx_send_sem,
    ctx_recv_sem,
    part_send_sem,
    part_recv_sem,
):
    rows, length, width = inputs_ref.shape
    head = weights.shape[2]
    seg = length // mp_count
    total = rows * length
    seg_total = rows * seg
    mode_count = table_ref.shape[0]
    my_dp = lax.axis_index("dp")
    my_mp = lax.axis_index("mp")
    right = lax.rem(my_dp + 1, dp_count)
    left = lax.rem(my_dp + dp_count - 1, dp_count)

    barrier = pltpu.get_barrier_semaphore()
    for neighbour in (left, right):
        pl.semaphore_signal(barrier, inc=1, device_id={"dp": neighbour}, device_id_type=MESH)
    for step in range(1, mp_count):
        pl.semaphore_signal(
            barrier,
            inc=1,
            device_id={"mp": lax.rem(my_mp + step, mp_count)},
            device_id_type=MESH,
        )

    load_inputs = pltpu.make_async_copy(inputs_hbm, inputs_ref, in_sem.at[0])
    load_inputs.start()
    load_cot = pltpu.make_async_copy(cot_hbm.at[pl.ds(0, rows)], cot_ref, in_sem.at[1])
    load_cot.start()
    depth = width // FORWARD_CHUNKS
    loads = []
    for which, source in enumerate((wq_hbm, wk_hbm, wv_hbm)):
        for chunk in range(FORWARD_CHUNKS):
            piece = pl.ds(chunk * depth, depth)
            load = pltpu.make_async_copy(
                source.at[piece], weights.at[which, piece], w_sem.at[which, chunk]
            )
            load.start()
            loads.append(load)

    def split(index):
        row = lax.rem(lax.div(index, seg), rows)
        place = lax.div(index, seg_total) * seg + lax.rem(index, seg)
        return row, place

    def per_row(row, ref):
        value = jnp.zeros_like(row)
        for r in range(rows):
            value = jnp.where(row == r, ref[r], value)
        return value

    col_row, col_place = split(lax.broadcasted_iota(jnp.int32, (total, 1), 0))
    lane_row, lane_place = split(lax.broadcasted_iota(jnp.int32, (1, total), 1))
    natural_lane = lax.broadcasted_iota(jnp.int32, (total, total), 1)
    permute = (natural_lane == col_row * length + col_place).astype(F32).astype(BF16)
    col_len = per_row(col_row, lengths_ref)
    key_ok = (col_row == lane_row) & (lane_place < jnp.maximum(col_len, 1))
    query_ok = col_place < col_len

    def span_column(r, start, count):
        flags = jnp.broadcast_to(span_ref[r : r + 1, :], (count, length))
        place = lax.broadcasted_iota(jnp.int32, (count, length), 0) + start
        lane = lax.broadcasted_iota(jnp.int32, (count, length), 1)
        return jnp.sum(
            jnp.where((place == lane) & (flags == 1), 1.0, 0.0), axis=1, keepdims=True
        )

    span_natural = [span_column(r, 0, length) for r in range(rows)]
    denoiser_col = [jnp.full((1, 1), denoiser_ref[r], jnp.int32) for r in range(rows)]

    load_inputs.wait()
    norm_width = width // NORM_CHUNKS
    squares = jnp.zeros((total, 1), F32)
    for chunk in range(NORM_CHUNKS):
        columns = pl.ds(chunk * norm_width, norm_width)
        sentinel = sentinel_ref[:, columns].astype(F32)
        table = table_ref[:, columns].astype(F32)
        pieces = []
        for r in range(rows):
            mode_row = jnp.zeros((1, norm_width), F32)
            for mode in range(mode_count):
                mode_row = jnp.where(denoiser_col[r] == mode, table[mode : mode + 1], mode_row)
            plain = inputs_ref[r, :, columns].astype(F32) + mode_row
            pieces.append(jnp.where(span_natural[r] > 0.5, sentinel, plain).astype(BF16))
        shaped = matmul(permute, jnp.concatenate(pieces, axis=0))
        normed_ref[:, columns] = shaped
        squares += jnp.sum(shaped * shaped, axis=1, keepdims=True)
    inv_rms = lax.rsqrt(squares * (1.0 / width) + 1e-06)
    for chunk in range(NORM_CHUNKS):
        columns = pl.ds(chunk * norm_width, norm_width)
        normed = normed_ref[:, columns] * inv_rms
        normed_ref[:, columns] = normed
        normed_b_ref[:, columns] = normed.astype(BF16)

    pl.semaphore_wait(barrier, 2 + mp_count - 1)
    cot_copies = []
    for at, (slot, home) in enumerate(((rows, left), (rows + 1, right))):
        copy = pltpu.make_async_remote_copy(
            src_ref=cot_hbm.at[slot],
            dst_ref=cot_recv.at[at],
            send_sem=cot_send_sem.at[at],
            recv_sem=cot_recv_sem.at[at],
            device_id={"dp": home},
            device_id_type=MESH,
        )
        copy.start()
        cot_copies.append(copy)

    projected = []
    for which in range(3):
        result = jnp.zeros((total, head), F32)
        for chunk in range(FORWARD_CHUNKS):
            loads[which * FORWARD_CHUNKS + chunk].wait()
            piece = pl.ds(chunk * depth, depth)
            result += matmul(normed_b_ref[:, piece], weights[which, piece, :])
        projected.append(result)
    query, key, value = [result.astype(BF16) for result in projected]

    factor = 1.0 / math.sqrt(head)
    scores = jnp.where(key_ok, matmul(query, key, NT) * factor, -jnp.inf)
    exp_scores = jnp.exp(scores - jnp.max(scores, axis=1, keepdims=True))
    soft = exp_scores / jnp.sum(exp_scores, axis=1, keepdims=True)
    soft_b = soft.astype(BF16)
    context = jnp.where(query_ok, matmul(soft_b, value), 0.0).astype(BF16)
    context = matmul(permute, context, TN)

    def moves(r, offset):
        return jnp.full((1, 1), move_ref[r], jnp.int32) == offset

    for at, offset in enumerate((1, -1)):
        leaving = jnp.zeros((length, head), F32)
        for r in range(rows):
            leaving = jnp.where(moves(r, offset), context[r * length : (r + 1) * length], leaving)
        ctx_send[at] = leaving.astype(BF16)
    ctx_copies = []
    for at, (slot, target) in enumerate(((rows, right), (rows + 1, left))):
        copy = pltpu.make_async_remote_copy(
            src_ref=ctx_send.at[at],
            dst_ref=context_ref.at[slot],
            send_sem=ctx_send_sem.at[at],
            recv_sem=ctx_recv_sem.at[at],
            device_id={"dp": target},
            device_id_type=MESH,
        )
        copy.start()
        ctx_copies.append(copy)
    for r in range(rows):
        own = jnp.where(moves(r, 0), context[r * length : (r + 1) * length], 0.0)
        context_ref[r] = own.astype(BF16)

    load_cot.wait()
    for copy in cot_copies:
        copy.wait()
    from_right = cot_recv[0].astype(F32)
    from_left = cot_recv[1].astype(F32)
    pieces = []
    for r in range(rows):
        moved = jnp.where(moves(r, 1), from_right, from_left)
        pieces.append(jnp.where(moves(r, 0), cot_ref[r].astype(F32), moved).astype(BF16))
    grad_out = matmul(permute, jnp.concatenate(pieces, axis=0))
    grad_out = jnp.where(query_ok, grad_out, 0.0).astype(BF16)

    grad_value = matmul(soft_b, grad_out, TN).astype(BF16)
    grad_soft = matmul(grad_out, value, NT)
    row_inner = jnp.sum(soft * grad_soft, axis=1, keepdims=True)
    grad_scores = (soft * (grad_soft - row_inner) * factor).astype(BF16)
    grad_query = matmul(grad_scores, key).astype(BF16)
    grad_key = matmul(grad_scores, query, TN).astype(BF16)
    gradients = (grad_query, grad_key, grad_value)
    inner = jnp.zeros((total, 1), F32)
    for gradient, result in zip(gradients, projected):
        inner += jnp.sum(gradient.astype(F32) * result, axis=1, keepdims=True)
    inner = inner * (1.0 / width)

    back_width = width // BACK_CHUNKS
    half = back_width // 2
    part_copies = []
    for chunk in range(BACK_CHUNKS):
        piece = pl.ds(chunk * back_width, back_width)
        head_grad = matmul(gradients[0], weights[0, piece, :], NT)
        head_grad += matmul(gradients[1], weights[1, piece, :], NT)
        head_grad += matmul(gradients[2], weights[2, piece, :], NT)
        head_part = (head_grad - normed_ref[:, piece] * inner) * inv_rms
        for s in range(mp_count):
            block = head_part[s * seg_total : (s + 1) * seg_total]
            stacked = jnp.concatenate([block[:, :half], block[:, half:]], axis=0)
            part_send[chunk, s] = stacked.astype(BF16)
        copies = []
        for step in range(1, mp_count):
            peer = lax.rem(my_mp + step, mp_count)
            copy = pltpu.make_async_remote_copy(
                src_ref=part_send.at[chunk, peer],
                dst_ref=part_recv.at[chunk, step - 1],
                send_sem=part_send_sem.at[chunk, step - 1],
                recv_sem=part_recv_sem.at[chunk, step - 1],
                device_id={"mp": peer},
                device_id_type=MESH,
            )
            copy.start()
            copies.append(copy)
        part_copies.append(copies)

    span_own = jnp.concatenate(
        [span_column(r, my_mp * seg, seg) for r in range(rows)], axis=0
    )
    for chunk in range(BACK_CHUNKS):
        summed = part_send[chunk, my_mp].astype(F32)
        for step in range(1, mp_count):
            part_copies[chunk][step - 1].wait_recv()
            summed += part_recv[chunk, step - 1].astype(F32)
        for part in range(2):
            block = jnp.where(
                span_own > 0.5, 0.0, summed[part * seg_total : (part + 1) * seg_total]
            ).astype(BF16)
            columns = pl.ds(chunk * back_width + part * half, half)
            for r in range(rows):
                grad_ref[r, :, columns] = block[r * seg : (r + 1) * seg]

    for copies in part_copies:
        for copy in copies:
            copy.wait_send()
    for copy in ctx_copies:
        copy.wait()


def shards(
    inputs,
    denoiser,
    span_mask,
    lengths,
    move_plan,
    mode_table,
    sentinel,
    w_query,
    w_key,
    w_value,
    cotangent,
):
    rows, length, width = inputs.shape
    head = w_query.shape[1]
    dp_count = lax.axis_size("dp")
    mp_count = lax.axis_size("mp")
    seg = length // mp_count
    total = rows * length
    block = (2 * rows * seg, width // BACK_CHUNKS // 2)
    smem = pl.BlockSpec(memory_space=pltpu.SMEM)
    vmem = pl.BlockSpec(memory_space=pltpu.VMEM)
    anywhere = pl.BlockSpec(memory_space=pltpu.HBM)
    dma = pltpu.SemaphoreType.DMA
    return pl.pallas_call(
        functools.partial(kernel, dp_count, mp_count),
        out_shape=(
            jax.ShapeDtypeStruct(cotangent.shape, BF16),
            jax.ShapeDtypeStruct((rows, seg, width), BF16),
        ),
        in_specs=[smem, smem, smem, vmem, vmem, vmem] + [anywhere] * 5,
        out_specs=(vmem, vmem),
        scratch_shapes=[
            pltpu.VMEM((rows, length, width), BF16),
            pltpu.VMEM((rows, length, head), BF16),
            pltpu.VMEM((3, width, head), BF16),
            pltpu.VMEM((total, width), F32),
            pltpu.VMEM((total, width), BF16),
            pltpu.VMEM((2, length, head), BF16),
            pltpu.VMEM((2, length, head), BF16),
            pltpu.VMEM((BACK_CHUNKS, mp_count) + block, BF16),
            pltpu.VMEM((BACK_CHUNKS, mp_count - 1) + block, BF16),
            dma((2,)),
            dma((3, FORWARD_CHUNKS)),
            dma((2,)),
            dma((2,)),
            dma((2,)),
            dma((2,)),
            dma((BACK_CHUNKS, mp_count - 1)),
            dma((BACK_CHUNKS, mp_count - 1)),
        ],
        compiler_params=pltpu.CompilerParams(
            collective_id=0, has_side_effects=True, vmem_limit_bytes=48 * 1024 * 1024
        ),
        cost_estimate=pl.CostEstimate(
            flops=4 * total * width * 3 * head,
            bytes_accessed=2 * 3 * width * head + 4 * total * width,
            transcendentals=total * total,
        ),
    )(
        denoiser,
        lengths,
        move_plan,
        span_mask,
        mode_table,
        sentinel.reshape(1, width),
        inputs,
        cotangent,
        w_query,
        w_key,
        w_value,
    )


def solution(mesh):
    return jax.shard_map(
        shards,
        mesh=mesh,
        in_specs=(
            P("dp", None, None),
            P("dp"),
            P("dp", None),
            P("dp"),
            P("dp"),
            P(),
            P(),
            P(None, "mp"),
            P(None, "mp"),
            P(None, "mp"),
            P("dp", None, "mp"),
        ),
        out_specs=(P("dp", None, "mp"), P("dp", "mp", None)),
        check_vma=False,
    )
```

time: 93.3 us -> 28.8 us (0.31)
  waiting for transfers between devices: 41.5 us -> 0 us
  between operations: 18.7 us -> 0.66 us
  Pallas kernels: 0 us -> 17.4 us
  other arithmetic: 14.8 us -> 0 us
  starting transfers between devices: 8.76 us -> 0 us
  local copies, waits for them, and re-layouts: 1.89 us -> 10.2 us
  matrix products: 7.2 us -> 0 us
    unnamed x2 -> x0, waiting for transfers between devices: 34.8 us -> none
    pallas_call x0 -> x1, Pallas kernels: none -> 17.4 us  [shards(): pl.pallas_call(functools.partial(kernel, dp_count, mp_count), out_shape=(...]
    ppermute x6 -> x0, starting transfers between devices: 8.72 us -> none  [shifted(): lax.ppermute(array, axis, [(i, (i + by) % devices) for i in range(devices)])]
    unnamed x15 -> x20, local copies, waits for them, and re-layouts: 1.76 us -> 9.53 us
    dot_general x12 -> x0, matrix products: 7.2 us -> none  [the longest x3 4.11 us: project_back(): lax.dot_general(flat_grad, weight, (((1,), (1,)), ((), ())), preferred_el...]
    ppermute x6 -> x0, waiting for transfers between devices: 6.73 us -> none  [shifted(): lax.ppermute(array, axis, [(i, (i + by) % devices) for i in range(devices)])]
    select_n x3 -> x0, other arithmetic: 3.79 us -> none  [the longest x1 1.62 us: shards(): jnp.where((span_piece == 1)[:, :, None], jnp.zeros_like(summed), summed)]
    convert_element_type x5 -> x0, other arithmetic: 2.93 us -> none  [the longest x1 1.05 us: shards(): shaped = jnp.where(span_flag, sentinel.astype(jnp.float32)[None, None, :]...]
  transfers between devices with their start and end apart: 7 -> 0, of which waited for: 4 -> 0; matrix products, arithmetic and copies ran while one was open for 5% -> 0% of each run, Pallas kernels for 0% -> 0%
where the time goes in v1:
time: 28.8 us; the launch traced here: 28.3 us
  Pallas kernels  17.4 us (60%)
  local copies, waits for them, and re-layouts  10.2 us (35%)
  between operations  0.66 us (2%)
    pallas_call x1, Pallas kernels, shards(): pl.pallas_call(functools.partial(kernel, dp_count, mp_count), out_shape=(...  17.4 us
    unnamed x20, local copies, waits for them, and re-layouts  9.53 us
    reshape x1, local copies, waits for them, and re-layouts, shards(): sentinel.reshape(1, width)  0.71 us

profile of v1, /device:TPU:0, one launch (start us, length us, event | category | flops | bytes accessed | tf_op | source)
XLA Modules:
  0.0 28.3 jit_solution(11985888806490991384)
XLA Ops:
  0.6 0.7 %reshape.7.sentinel_ref = bf16[1,4096]{1,0:T(2,128)(2,1)S(1)} reshape(bf16[4096]{0:T(1024)(128)(2,1)} %param.17) | data formatting | bytes 16384 | tf_op jit(solution)/shard_map/reshape | solution.py:348
  1.3 0.0 copy-start
  1.4 1.6 %copy-done = bf16[4096,256]{1,0:T(8,128)(2,1)S(1)} copy-done((bf16[4096,256]{1,0:T(8,128)(2,1)S(1)}, bf16[4096,256]{1,0:T(8,128)(2,1)}, u32[]{:S(2)}) %copy-start) | copy-done | bytes 2097176
  2.9 0.0 copy-start.1
  2.9 1.6 %copy-done.1 = bf16[4096,256]{1,0:T(8,128)(2,1)S(1)} copy-done((bf16[4096,256]{1,0:T(8,128)(2,1)S(1)}, bf16[4096,256]{1,0:T(8,128)(2,1)}, u32[]{:S(2)}) %copy-start.1) | copy-done | bytes 2097176
  4.5 0.0 copy-start.2
  4.5 0.9 %copy-done.2 = bf16[2,16,4096]{2,1,0:T(8,128)(2,1)S(1)} copy-done((bf16[2,16,4096]{2,1,0:T(8,128)(2,1)S(1)}, bf16[2,16,4096]{2,1,0:T(8,128)(2,1)}, u32[]{:S(2)}) %copy-start.2) | copy-done | bytes 262168
  5.5 0.0 copy-start.3
  5.5 0.8 %copy-done.3 = bf16[3,4096]{1,0:T(4,128)(2,1)S(1)} copy-done((bf16[3,4096]{1,0:T(4,128)(2,1)S(1)}, bf16[3,4096]{1,0:T(4,128)(2,1)}, u32[]{:S(2)}) %copy-start.3) | copy-done | bytes 24600
  6.2 0.0 copy-start.4
  6.2 0.8 %copy-done.4 = bf16[4,16,256]{2,1,0:T(8,128)(2,1)S(1)} copy-done((bf16[4,16,256]{2,1,0:T(8,128)(2,1)S(1)}, bf16[4,16,256]{2,1,0:T(8,128)(2,1)}, u32[]{:S(2)}) %copy-start.4) | copy-done | bytes 32792
  7.0 0.0 copy-start.5
  7.0 0.7 %copy-done.5 = s32[2,16]{1,0:T(2,128)S(1)} copy-done((s32[2,16]{1,0:T(2,128)S(1)}, s32[2,16]{1,0:T(2,128)}, u32[]{:S(2)}) %copy-start.5) | copy-done | bytes 152
  7.7 0.0 copy-start.6
  7.7 0.7 %copy-done.6 = s32[2]{0:T(128)S(1)} copy-done((s32[2]{0:T(128)S(1)}, s32[2]{0:T(128)}, u32[]{:S(2)}) %copy-start.6) | copy-done | bytes 32
  8.3 0.0 copy-start.7
  8.3 0.7 %copy-done.7 = s32[2]{0:T(128)S(1)} copy-done((s32[2]{0:T(128)S(1)}, s32[2]{0:T(128)}, u32[]{:S(2)}) %copy-start.7) | copy-done | bytes 32
  9.0 0.0 copy-start.8
  9.0 0.7 %copy-done.8 = s32[2]{0:T(128)S(1)} copy-done((s32[2]{0:T(128)S(1)}, s32[2]{0:T(128)}, u32[]{:S(2)}) %copy-start.8) | copy-done | bytes 32
  9.6 17.4 %shard_map.122 = (bf16[4,16,256]{2,1,0:T(8,128)(2,1)S(1)}, bf16[2,4,4096]{2,1,0:T(4,128)(2,1)S(1)}) custom-call(s32[2]{0:T(128)S(1)} %copy-done.6, s32[2]{0:T(128)S(1)} %copy-done.7, s32[2]{0:T(128)S(1)} %copy-done.8, s32[2,16]{1,0:T(2,128)S(1)} %copy-done.5, bf16[3,4096]{1,0:T(4,128)(2,1)S(1)} %copy-done.3, bf16[1,4096]{1,0:T(2,128)(2,1)S(1)} %reshape.7.sentinel_ref, ...), custom_call_target="tpu_custom_call" | custom-call | flops 402653184 | bytes 6815744 | tf_op jit(solution)/shard_map/pallas_call | solution.py:307
  27.1 0.6 %copy.15 = bf16[4,16,256]{2,1,0:T(8,128)(2,1)} copy(bf16[4,16,256]{2,1,0:T(8,128)(2,1)S(1)} %get-tuple-element.4) | data formatting | bytes 65536
  27.7 0.6 %copy.16 = bf16[2,4,4096]{2,1,0:T(4,128)(2,1)} copy(bf16[2,4,4096]{2,1,0:T(4,128)(2,1)S(1)} %get-tuple-element.5) | data formatting | bytes 131072
Async XLA Ops:
  1.3 1.6 %copy-start = (bf16[4096,256]{1,0:T(8,128)(2,1)S(1)}, bf16[4096,256]{1,0:T(8,128)(2,1)}, u32[]{:S(2)}) copy-start(bf16[4096,256]{1,0:T(8,128)(2,1)} %wq_hbm.1) | copy-start | bytes 6291460
  2.9 1.6 %copy-start.1 = (bf16[4096,256]{1,0:T(8,128)(2,1)S(1)}, bf16[4096,256]{1,0:T(8,128)(2,1)}, u32[]{:S(2)}) copy-start(bf16[4096,256]{1,0:T(8,128)(2,1)} %wk_hbm.1) | copy-start | bytes 6291460
  4.5 0.9 %copy-start.2 = (bf16[2,16,4096]{2,1,0:T(8,128)(2,1)S(1)}, bf16[2,16,4096]{2,1,0:T(8,128)(2,1)}, u32[]{:S(2)}) copy-start(bf16[2,16,4096]{2,1,0:T(8,128)(2,1)} %inputs_hbm.1) | copy-start | bytes 786436
  5.5 0.8 %copy-start.3 = (bf16[3,4096]{1,0:T(4,128)(2,1)S(1)}, bf16[3,4096]{1,0:T(4,128)(2,1)}, u32[]{:S(2)}) copy-start(bf16[3,4096]{1,0:T(4,128)(2,1)} %table_ref.1) | copy-start | bytes 73732
  6.2 0.8 %copy-start.4 = (bf16[4,16,256]{2,1,0:T(8,128)(2,1)S(1)}, bf16[4,16,256]{2,1,0:T(8,128)(2,1)}, u32[]{:S(2)}) copy-start(bf16[4,16,256]{2,1,0:T(8,128)(2,1)} %cot_hbm.1) | copy-start | bytes 98308
  7.0 0.7 %copy-start.5 = (s32[2,16]{1,0:T(2,128)S(1)}, s32[2,16]{1,0:T(2,128)}, u32[]{:S(2)}) copy-start(s32[2,16]{1,0:T(2,128)} %span_ref.1) | copy-start | bytes 388
  7.7 0.7 %copy-start.6 = (s32[2]{0:T(128)S(1)}, s32[2]{0:T(128)}, u32[]{:S(2)}) copy-start(s32[2]{0:T(128)} %denoiser_ref.1) | copy-start | bytes 28
  8.3 0.7 %copy-start.7 = (s32[2]{0:T(128)S(1)}, s32[2]{0:T(128)}, u32[]{:S(2)}) copy-start(s32[2]{0:T(128)} %lengths_ref.1) | copy-start | bytes 28
  9.0 0.7 %copy-start.8 = (s32[2]{0:T(128)S(1)}, s32[2]{0:T(128)}, u32[]{:S(2)}) copy-start(s32[2]{0:T(128)} %move_ref.1) | copy-start | bytes 28

commit v2 on v1

--- a/solution.py
+++ b/solution.py
@@ -17,7 +17,8 @@
 
 FORWARD_CHUNKS = 4
 BACK_CHUNKS = 4
-NORM_CHUNKS = 8
+NORM_CHUNKS = 4
+LANES = 128
 
 
 def matmul(a, b, dims=NN):
@@ -27,12 +28,12 @@
 def kernel(
     dp_count,
     mp_count,
-    denoiser_ref,
-    lengths_ref,
-    move_ref,
-    span_ref,
-    table_ref,
-    sentinel_ref,
+    denoiser_hbm,
+    lengths_hbm,
+    move_hbm,
+    span_hbm,
+    table_hbm,
+    sentinel_hbm,
     inputs_hbm,
     cot_hbm,
     wq_hbm,
@@ -40,6 +41,12 @@
     wv_hbm,
     context_ref,
     grad_ref,
+    denoiser_ref,
+    lengths_ref,
+    move_ref,
+    span_ref,
+    table_ref,
+    sentinel_ref,
     inputs_ref,
     cot_ref,
     weights,
@@ -49,6 +56,7 @@
     ctx_send,
     part_send,
     part_recv,
+    small_sem,
     in_sem,
     w_sem,
     cot_send_sem,
@@ -80,6 +88,20 @@
             device_id_type=MESH,
         )
 
+    small_loads = []
+    for at, (source, target) in enumerate(
+        (
+            (denoiser_hbm, denoiser_ref),
+            (lengths_hbm, lengths_ref),
+            (move_hbm, move_ref),
+            (span_hbm, span_ref),
+            (table_hbm, table_ref),
+            (sentinel_hbm, sentinel_ref),
+        )
+    ):
+        load = pltpu.make_async_copy(source, target, small_sem.at[at])
+        load.start()
+        small_loads.append(load)
     load_inputs = pltpu.make_async_copy(inputs_hbm, inputs_ref, in_sem.at[0])
     load_inputs.start()
     load_cot = pltpu.make_async_copy(cot_hbm.at[pl.ds(0, rows)], cot_ref, in_sem.at[1])
@@ -95,6 +117,9 @@
             load.start()
             loads.append(load)
 
+    for load in small_loads:
+        load.wait()
+
     def split(index):
         row = lax.rem(lax.div(index, seg), rows)
         place = lax.div(index, seg_total) * seg + lax.rem(index, seg)
@@ -130,7 +155,9 @@
     squares = jnp.zeros((total, 1), F32)
     for chunk in range(NORM_CHUNKS):
         columns = pl.ds(chunk * norm_width, norm_width)
-        sentinel = sentinel_ref[:, columns].astype(F32)
+        lines = norm_width // LANES
+        lines_f32 = sentinel_ref[pl.ds(chunk * lines, lines), :].astype(F32)
+        sentinel = jnp.concatenate([lines_f32[i : i + 1] for i in range(lines)], axis=1)
         table = table_ref[:, columns].astype(F32)
         pieces = []
         for r in range(rows):
@@ -178,32 +205,8 @@
     exp_scores = jnp.exp(scores - jnp.max(scores, axis=1, keepdims=True))
     soft = exp_scores / jnp.sum(exp_scores, axis=1, keepdims=True)
     soft_b = soft.astype(BF16)
-    context = jnp.where(query_ok, matmul(soft_b, value), 0.0).astype(BF16)
-    context = matmul(permute, context, TN)
-
     def moves(r, offset):
         return jnp.full((1, 1), move_ref[r], jnp.int32) == offset
-
-    for at, offset in enumerate((1, -1)):
-        leaving = jnp.zeros((length, head), F32)
-        for r in range(rows):
-            leaving = jnp.where(moves(r, offset), context[r * length : (r + 1) * length], leaving)
-        ctx_send[at] = leaving.astype(BF16)
-    ctx_copies = []
-    for at, (slot, target) in enumerate(((rows, right), (rows + 1, left))):
-        copy = pltpu.make_async_remote_copy(
-            src_ref=ctx_send.at[at],
-            dst_ref=context_ref.at[slot],
-            send_sem=ctx_send_sem.at[at],
-            recv_sem=ctx_recv_sem.at[at],
-            device_id={"dp": target},
-            device_id_type=MESH,
-        )
-        copy.start()
-        ctx_copies.append(copy)
-    for r in range(rows):
-        own = jnp.where(moves(r, 0), context[r * length : (r + 1) * length], 0.0)
-        context_ref[r] = own.astype(BF16)
 
     load_cot.wait()
     for copy in cot_copies:
@@ -257,6 +260,30 @@
             copies.append(copy)
         part_copies.append(copies)
 
+    context = jnp.where(query_ok, matmul(soft_b, value), 0.0).astype(BF16)
+    context = matmul(permute, context, TN)
+
+    for at, offset in enumerate((1, -1)):
+        leaving = jnp.zeros((length, head), F32)
+        for r in range(rows):
+            leaving = jnp.where(moves(r, offset), context[r * length : (r + 1) * length], leaving)
+        ctx_send[at] = leaving.astype(BF16)
+    ctx_copies = []
+    for at, (slot, target) in enumerate(((rows, right), (rows + 1, left))):
+        copy = pltpu.make_async_remote_copy(
+            src_ref=ctx_send.at[at],
+            dst_ref=context_ref.at[slot],
+            send_sem=ctx_send_sem.at[at],
+            recv_sem=ctx_recv_sem.at[at],
+            device_id={"dp": target},
+            device_id_type=MESH,
+        )
+        copy.start()
+        ctx_copies.append(copy)
+    for r in range(rows):
+        own = jnp.where(moves(r, 0), context[r * length : (r + 1) * length], 0.0)
+        context_ref[r] = own.astype(BF16)
+
     span_own = jnp.concatenate(
         [span_column(r, my_mp * seg, seg) for r in range(rows)], axis=0
     )
@@ -300,7 +327,6 @@
     seg = length // mp_count
     total = rows * length
     block = (2 * rows * seg, width // BACK_CHUNKS // 2)
-    smem = pl.BlockSpec(memory_space=pltpu.SMEM)
     vmem = pl.BlockSpec(memory_space=pltpu.VMEM)
     anywhere = pl.BlockSpec(memory_space=pltpu.HBM)
     dma = pltpu.SemaphoreType.DMA
@@ -310,9 +336,15 @@
             jax.ShapeDtypeStruct(cotangent.shape, BF16),
             jax.ShapeDtypeStruct((rows, seg, width), BF16),
         ),
-        in_specs=[smem, smem, smem, vmem, vmem, vmem] + [anywhere] * 5,
+        in_specs=[anywhere] * 11,
         out_specs=(vmem, vmem),
         scratch_shapes=[
+            pltpu.SMEM((rows,), jnp.int32),
+            pltpu.SMEM((rows,), jnp.int32),
+            pltpu.SMEM((rows,), jnp.int32),
+            pltpu.VMEM((rows, length), jnp.int32),
+            pltpu.VMEM(mode_table.shape, BF16),
+            pltpu.VMEM((width // LANES, LANES), BF16),
             pltpu.VMEM((rows, length, width), BF16),
             pltpu.VMEM((rows, length, head), BF16),
             pltpu.VMEM((3, width, head), BF16),
@@ -322,6 +354,7 @@
             pltpu.VMEM((2, length, head), BF16),
             pltpu.VMEM((BACK_CHUNKS, mp_count) + block, BF16),
             pltpu.VMEM((BACK_CHUNKS, mp_count - 1) + block, BF16),
+            dma((6,)),
             dma((2,)),
             dma((3, FORWARD_CHUNKS)),
             dma((2,)),
@@ -332,7 +365,7 @@
             dma((BACK_CHUNKS, mp_count - 1)),
         ],
         compiler_params=pltpu.CompilerParams(
-            collective_id=0, has_side_effects=True, vmem_limit_bytes=48 * 1024 * 1024
+            collective_id=0, has_side_effects=True, vmem_limit_bytes=64 * 1024 * 1024
         ),
         cost_estimate=pl.CostEstimate(
             flops=4 * total * width * 3 * head,
@@ -345,7 +378,7 @@
         move_plan,
         span_mask,
         mode_table,
-        sentinel.reshape(1, width),
+        sentinel.reshape(width // LANES, LANES),
         inputs,
         cotangent,
         w_query,

time: 28.8 us -> 23.6 us (0.82)
  local copies, waits for them, and re-layouts: 10.2 us -> 2.87 us
  Pallas kernels: 17.4 us -> 19.8 us
    unnamed x20 -> x2, local copies, waits for them, and re-layouts: 9.53 us -> 2.87 us
    pallas_call x1, Pallas kernels: 17.4 us -> 19.8 us  [shards(): pl.pallas_call(functools.partial(kernel, dp_count, mp_count), out_shape=(...]
    reshape x1 -> x0, local copies, waits for them, and re-layouts: 0.71 us -> none  [shards(): sentinel.reshape(1, width)]
where the time goes in v2:
time: 23.6 us; the launch traced here: 23.3 us
  Pallas kernels  19.8 us (84%)
  local copies, waits for them, and re-layouts  2.87 us (12%)
  between operations  0.64 us (3%)
    pallas_call x1, Pallas kernels, shards(): pl.pallas_call(functools.partial(kernel, dp_count, mp_count), out_shape=(...  19.8 us
    unnamed x2, local copies, waits for them, and re-layouts  2.87 us

profile of v2, /device:TPU:0, one launch (start us, length us, event | category | flops | bytes accessed | tf_op | source)
XLA Modules:
  0.0 23.3 jit_solution(3477094250287913422)
XLA Ops:
  0.6 19.8 %shard_map.122 = (bf16[4,16,256]{2,1,0:T(8,128)(2,1)}, bf16[2,4,4096]{2,1,0:T(4,128)(2,1)}) custom-call(s32[2]{0:T(128)} %denoiser_hbm.1, s32[2]{0:T(128)} %lengths_hbm.1, s32[2]{0:T(128)} %move_hbm.1, s32[2,16]{1,0:T(2,128)} %span_hbm.1, bf16[3,4096]{1,0:T(4,128)(2,1)} %table_hbm.1, bf16[32,128]{1,0:T(8,128)(2,1)} %bitcast.1, ...), custom_call_target="tpu_custom_call" | custom-call | flops 402653184 | bytes 6815744 | tf_op jit(solution)/shard_map/pallas_call | solution.py:333
  20.5 1.4 %copy.15 = bf16[4,16,256]{2,1,0:T(8,128)(2,1)} copy(bf16[4,16,256]{2,1,0:T(8,128)(2,1)} %get-tuple-element.4) | data formatting | bytes 65536
  21.9 1.5 %copy.16 = bf16[2,4,4096]{2,1,0:T(4,128)(2,1)} copy(bf16[2,4,4096]{2,1,0:T(4,128)(2,1)} %get-tuple-element.5) | data formatting | bytes 131072

commit v3 on v2

--- a/solution.py
+++ b/solution.py
@@ -333,8 +333,8 @@
     return pl.pallas_call(
         functools.partial(kernel, dp_count, mp_count),
         out_shape=(
-            jax.ShapeDtypeStruct(cotangent.shape, BF16),
-            jax.ShapeDtypeStruct((rows, seg, width), BF16),
+            pltpu.VMEM(cotangent.shape, BF16),
+            pltpu.VMEM((rows, seg, width), BF16),
         ),
         in_specs=[anywhere] * 11,
         out_specs=(vmem, vmem),
@@ -365,7 +365,7 @@
             dma((BACK_CHUNKS, mp_count - 1)),
         ],
         compiler_params=pltpu.CompilerParams(
-            collective_id=0, has_side_effects=True, vmem_limit_bytes=64 * 1024 * 1024
+            collective_id=0, has_side_effects=True, vmem_limit_bytes=48 * 1024 * 1024
         ),
         cost_estimate=pl.CostEstimate(
             flops=4 * total * width * 3 * head,
@@ -373,17 +373,22 @@
             transcendentals=total * total,
         ),
     )(
-        denoiser,
-        lengths,
-        move_plan,
-        span_mask,
-        mode_table,
-        sentinel.reshape(width // LANES, LANES),
-        inputs,
-        cotangent,
-        w_query,
-        w_key,
-        w_value,
+        *[
+            pltpu.with_memory_space_constraint(operand, pltpu.HBM)
+            for operand in (
+                denoiser,
+                lengths,
+                move_plan,
+                span_mask,
+                mode_table,
+                sentinel.reshape(width // LANES, LANES),
+                inputs,
+                cotangent,
+                w_query,
+                w_key,
+                w_value,
+            )
+        ]
     )
 
 

time: 23.6 us -> 21.2 us (0.90)
  local copies, waits for them, and re-layouts: 2.87 us -> 1.25 us
  Pallas kernels: 19.8 us -> 19.2 us
    unnamed x2, local copies, waits for them, and re-layouts: 2.87 us -> 1.25 us
    pallas_call x1, Pallas kernels: 19.8 us -> 19.2 us  [shards(): pl.pallas_call(functools.partial(kernel, dp_count, mp_count), out_shape=(...]
where the time goes in v3:
time: 21.2 us; the launch traced here: 21.1 us
  Pallas kernels  19.2 us (91%)
  local copies, waits for them, and re-layouts  1.25 us (6%)
  between operations  0.64 us (3%)
    pallas_call x1, Pallas kernels, shards(): pl.pallas_call(functools.partial(kernel, dp_count, mp_count), out_shape=(...  19.2 us
    unnamed x2, local copies, waits for them, and re-layouts  1.25 us

profile of v3, /device:TPU:0, one launch (start us, length us, event | category | flops | bytes accessed | tf_op | source)
XLA Modules:
  0.0 21.1 jit_solution(18042699411310160849)
XLA Ops:
  0.6 19.2 %shard_map.122 = (bf16[4,16,256]{2,1,0:T(8,128)(2,1)S(1)}, bf16[2,4,4096]{2,1,0:T(4,128)(2,1)S(1)}) custom-call(s32[2]{0:T(128)} %denoiser_hbm.1, s32[2]{0:T(128)} %lengths_hbm.1, s32[2]{0:T(128)} %move_hbm.1, s32[2,16]{1,0:T(2,128)} %span_hbm.1, bf16[3,4096]{1,0:T(4,128)(2,1)} %table_hbm.1, bf16[32,128]{1,0:T(8,128)(2,1)} %bitcast.1, ...), custom_call_target="tpu_custom_call" | custom-call | flops 402653184 | bytes 6815744 | tf_op jit(solution)/shard_map/pallas_call | solution.py:333
  19.8 0.6 %copy.15 = bf16[4,16,256]{2,1,0:T(8,128)(2,1)} copy(bf16[4,16,256]{2,1,0:T(8,128)(2,1)S(1)} %get-tuple-element.2) | data formatting | bytes 65536
  20.5 0.6 %copy.16 = bf16[2,4,4096]{2,1,0:T(4,128)(2,1)} copy(bf16[2,4,4096]{2,1,0:T(4,128)(2,1)S(1)} %get-tuple-element.3) | data formatting | bytes 131072

commit v4 on v3

--- a/solution.py
+++ b/solution.py
@@ -16,7 +16,7 @@
 NN = (((1,), (0,)), ((), ()))
 
 FORWARD_CHUNKS = 4
-BACK_CHUNKS = 4
+BACK_CHUNKS = 8
 NORM_CHUNKS = 4
 LANES = 128
 
@@ -190,27 +190,40 @@
         copy.start()
         cot_copies.append(copy)
 
-    projected = []
-    for which in range(3):
-        result = jnp.zeros((total, head), F32)
-        for chunk in range(FORWARD_CHUNKS):
-            loads[which * FORWARD_CHUNKS + chunk].wait()
-            piece = pl.ds(chunk * depth, depth)
-            result += matmul(normed_b_ref[:, piece], weights[which, piece, :])
-        projected.append(result)
-    query, key, value = [result.astype(BF16) for result in projected]
-
+    def project(which, chunk):
+        piece = pl.ds(chunk * depth, depth)
+        return matmul(normed_b_ref[:, piece], weights[which, piece, :])
+
+    query_f32 = jnp.zeros((total, head), F32)
+    key_f32 = jnp.zeros((total, head), F32)
+    for chunk in range(FORWARD_CHUNKS):
+        loads[chunk].wait()
+        query_f32 += project(0, chunk)
+    for chunk in range(FORWARD_CHUNKS):
+        loads[FORWARD_CHUNKS + chunk].wait()
+        key_f32 += project(1, chunk)
+    for chunk in range(FORWARD_CHUNKS):
+        loads[2 * FORWARD_CHUNKS + chunk].wait()
+    load_cot.wait()
+    for copy in cot_copies:
+        copy.wait()
+
+    query = query_f32.astype(BF16)
+    key = key_f32.astype(BF16)
     factor = 1.0 / math.sqrt(head)
     scores = jnp.where(key_ok, matmul(query, key, NT) * factor, -jnp.inf)
+    value_f32 = project(2, 0)
+    for chunk in range(1, FORWARD_CHUNKS):
+        value_f32 += project(2, chunk)
     exp_scores = jnp.exp(scores - jnp.max(scores, axis=1, keepdims=True))
     soft = exp_scores / jnp.sum(exp_scores, axis=1, keepdims=True)
     soft_b = soft.astype(BF16)
+    value = value_f32.astype(BF16)
+    projected = (query_f32, key_f32, value_f32)
+
     def moves(r, offset):
         return jnp.full((1, 1), move_ref[r], jnp.int32) == offset
 
-    load_cot.wait()
-    for copy in cot_copies:
-        copy.wait()
     from_right = cot_recv[0].astype(F32)
     from_left = cot_recv[1].astype(F32)
     pieces = []
@@ -307,6 +320,30 @@
         copy.wait()
 
 
+def store_kernel(context_ref, grad_ref, context_out, grad_out, sem):
+    copies = [
+        pltpu.make_async_copy(context_ref, context_out, sem.at[0]),
+        pltpu.make_async_copy(grad_ref, grad_out, sem.at[1]),
+    ]
+    for copy in copies:
+        copy.start()
+    for copy in copies:
+        copy.wait()
+
+
+def store(context, grad):
+    vmem = pl.BlockSpec(memory_space=pltpu.VMEM)
+    hbm = pl.BlockSpec(memory_space=pltpu.HBM)
+    return pl.pallas_call(
+        store_kernel,
+        out_shape=(pltpu.HBM(context.shape, BF16), pltpu.HBM(grad.shape, BF16)),
+        in_specs=[vmem, vmem],
+        out_specs=(hbm, hbm),
+        scratch_shapes=[pltpu.SemaphoreType.DMA((2,))],
+        compiler_params=pltpu.CompilerParams(vmem_limit_bytes=1024 * 1024),
+    )(context, grad)
+
+
 def shards(
     inputs,
     denoiser,
@@ -330,7 +367,7 @@
     vmem = pl.BlockSpec(memory_space=pltpu.VMEM)
     anywhere = pl.BlockSpec(memory_space=pltpu.HBM)
     dma = pltpu.SemaphoreType.DMA
-    return pl.pallas_call(
+    context, grad = pl.pallas_call(
         functools.partial(kernel, dp_count, mp_count),
         out_shape=(
             pltpu.VMEM(cotangent.shape, BF16),
@@ -390,6 +427,7 @@
             )
         ]
     )
+    return store(context, grad)
 
 
 def solution(mesh):

time: 21.2 us -> 21.1 us (level)
  local copies, waits for them, and re-layouts: 1.25 us -> 0 us
  Pallas kernels: 19.2 us -> 20.3 us
    unnamed x2 -> x0, local copies, waits for them, and re-layouts: 1.25 us -> none
    pallas_call x0 -> x1, Pallas kernels: none -> 0.66 us  [store(): pl.pallas_call(store_kernel, out_shape=(pltpu.HBM(context.shape, BF16), p...]
    pallas_call x1, Pallas kernels: 19.2 us -> 19.6 us  [shards(): pl.pallas_call(functools.partial(kernel, dp_count, mp_count), out_shape=(...]
where the time goes in v4:
time: 21.1 us; the launch traced here: 20.9 us
  Pallas kernels  20.3 us (96%)
  between operations  0.64 us (3%)
    pallas_call x1, Pallas kernels, shards(): pl.pallas_call(functools.partial(kernel, dp_count, mp_count), out_shape=(...  19.6 us
    pallas_call x1, Pallas kernels, store(): pl.pallas_call(store_kernel, out_shape=(pltpu.HBM(context.shape, BF16), p...  0.66 us

profile of v4, /device:TPU:0, one launch (start us, length us, event | category | flops | bytes accessed | tf_op | source)
XLA Modules:
  0.0 20.9 jit_solution(494374813040596552)
XLA Ops:
  0.6 19.6 %shard_map.122 = (bf16[4,16,256]{2,1,0:T(8,128)(2,1)S(1)}, bf16[2,4,4096]{2,1,0:T(4,128)(2,1)S(1)}) custom-call(s32[2]{0:T(128)} %denoiser_hbm.1, s32[2]{0:T(128)} %lengths_hbm.1, s32[2]{0:T(128)} %move_hbm.1, s32[2,16]{1,0:T(2,128)} %span_hbm.1, bf16[3,4096]{1,0:T(4,128)(2,1)} %table_hbm.1, bf16[32,128]{1,0:T(8,128)(2,1)} %bitcast.1, ...), custom_call_target="tpu_custom_call" | custom-call | flops 402653184 | bytes 6815744 | tf_op jit(solution)/shard_map/pallas_call | solution.py:370
  20.3 0.7 %shard_map.123 = (bf16[4,16,256]{2,1,0:T(8,128)(2,1)}, bf16[2,4,4096]{2,1,0:T(4,128)(2,1)}) custom-call(bf16[4,16,256]{2,1,0:T(8,128)(2,1)S(1)} %get-tuple-element.4.context_ref, bf16[2,4,4096]{2,1,0:T(4,128)(2,1)S(1)} %get-tuple-element.5.grad_ref), custom_call_target="tpu_custom_call" | custom-call | tf_op jit(solution)/shard_map/pallas_call | solution.py:337

commit v5 on v4

--- a/solution.py
+++ b/solution.py
@@ -56,6 +56,10 @@
     ctx_send,
     part_send,
     part_recv,
+    pair_recv,
+    pair_send,
+    mate_recv,
+    mate_sem,
     small_sem,
     in_sem,
     w_sem,
@@ -247,31 +251,81 @@
 
     back_width = width // BACK_CHUNKS
     half = back_width // 2
-    part_copies = []
-    for chunk in range(BACK_CHUNKS):
+    paired = mp_count == 4
+    mate = my_mp + 1 - 2 * lax.rem(my_mp, 2)
+    other = 2 - 2 * lax.div(my_mp, 2)
+    outer = (my_mp == 0) | (my_mp == mp_count - 1)
+
+    def remote(source, target, send_sem, recv_sem, peer):
+        return pltpu.make_async_remote_copy(
+            src_ref=source,
+            dst_ref=target,
+            send_sem=send_sem,
+            recv_sem=recv_sem,
+            device_id={"mp": peer},
+            device_id_type=MESH,
+        )
+
+    def back(chunk):
         piece = pl.ds(chunk * back_width, back_width)
         head_grad = matmul(gradients[0], weights[0, piece, :], NT)
         head_grad += matmul(gradients[1], weights[1, piece, :], NT)
         head_grad += matmul(gradients[2], weights[2, piece, :], NT)
+        return head_grad
+
+    def to_mate(chunk):
+        return remote(
+            part_send.at[chunk, pl.ds(other, 2)],
+            pair_recv.at[chunk],
+            part_send_sem.at[chunk, 0],
+            part_recv_sem.at[chunk, 0],
+            mate,
+        )
+
+    def from_inner(chunk, j):
+        return remote(
+            pair_send.at[chunk, j],
+            part_recv.at[chunk, 0],
+            part_send_sem.at[chunk, 1 + j],
+            part_recv_sem.at[chunk, 1],
+            other + j,
+        )
+
+    def direct(chunk, step):
+        peer = lax.rem(my_mp + step, mp_count)
+        return remote(
+            part_send.at[chunk, peer],
+            part_recv.at[chunk, step - 1],
+            part_send_sem.at[chunk, step - 1],
+            part_recv_sem.at[chunk, step - 1],
+            peer,
+        )
+
+    head_grad = back(0)
+    for chunk in range(BACK_CHUNKS):
+        piece = pl.ds(chunk * back_width, back_width)
+        following = back(chunk + 1) if chunk + 1 < BACK_CHUNKS else None
         head_part = (head_grad - normed_ref[:, piece] * inner) * inv_rms
         for s in range(mp_count):
             block = head_part[s * seg_total : (s + 1) * seg_total]
             stacked = jnp.concatenate([block[:, :half], block[:, half:]], axis=0)
             part_send[chunk, s] = stacked.astype(BF16)
-        copies = []
-        for step in range(1, mp_count):
-            peer = lax.rem(my_mp + step, mp_count)
-            copy = pltpu.make_async_remote_copy(
-                src_ref=part_send.at[chunk, peer],
-                dst_ref=part_recv.at[chunk, step - 1],
-                send_sem=part_send_sem.at[chunk, step - 1],
-                recv_sem=part_recv_sem.at[chunk, step - 1],
-                device_id={"mp": peer},
-                device_id_type=MESH,
-            )
-            copy.start()
-            copies.append(copy)
-        part_copies.append(copies)
+        if paired:
+
+            @pl.when(outer)
+            def _():
+                to_mate(chunk).start()
+
+        else:
+            for step in range(1, mp_count):
+                direct(chunk, step).start()
+        head_grad = following
+
+    if paired:
+        mate_copy = remote(
+            part_send.at[:, mate], mate_recv, mate_sem.at[0], mate_sem.at[1], mate
+        )
+        mate_copy.start()
 
     context = jnp.where(query_ok, matmul(soft_b, value), 0.0).astype(BF16)
     context = matmul(permute, context, TN)
@@ -297,14 +351,33 @@
         own = jnp.where(moves(r, 0), context[r * length : (r + 1) * length], 0.0)
         context_ref[r] = own.astype(BF16)
 
+    if paired:
+
+        @pl.when(jnp.logical_not(outer))
+        def _():
+            for chunk in range(BACK_CHUNKS):
+                to_mate(chunk).wait_recv()
+                for j in range(2):
+                    partial = part_send[chunk, other + j].astype(F32)
+                    partial += pair_recv[chunk, j].astype(F32)
+                    pair_send[chunk, j] = partial.astype(BF16)
+                    from_inner(chunk, j).start()
+
+        mate_copy.wait_recv()
+
     span_own = jnp.concatenate(
         [span_column(r, my_mp * seg, seg) for r in range(rows)], axis=0
     )
     for chunk in range(BACK_CHUNKS):
         summed = part_send[chunk, my_mp].astype(F32)
-        for step in range(1, mp_count):
-            part_copies[chunk][step - 1].wait_recv()
-            summed += part_recv[chunk, step - 1].astype(F32)
+        if paired:
+            summed += mate_recv[chunk].astype(F32)
+            from_inner(chunk, 0).wait_recv()
+            summed += part_recv[chunk, 0].astype(F32)
+        else:
+            for step in range(1, mp_count):
+                direct(chunk, step).wait_recv()
+                summed += part_recv[chunk, step - 1].astype(F32)
         for part in range(2):
             block = jnp.where(
                 span_own > 0.5, 0.0, summed[part * seg_total : (part + 1) * seg_total]
@@ -313,9 +386,24 @@
             for r in range(rows):
                 grad_ref[r, :, columns] = block[r * seg : (r + 1) * seg]
 
-    for copies in part_copies:
-        for copy in copies:
-            copy.wait_send()
+    if paired:
+        mate_copy.wait_send()
+
+        @pl.when(outer)
+        def _():
+            for chunk in range(BACK_CHUNKS):
+                to_mate(chunk).wait_send()
+
+        @pl.when(jnp.logical_not(outer))
+        def _():
+            for chunk in range(BACK_CHUNKS):
+                for j in range(2):
+                    from_inner(chunk, j).wait_send()
+
+    else:
+        for chunk in range(BACK_CHUNKS):
+            for step in range(1, mp_count):
+                direct(chunk, step).wait_send()
     for copy in ctx_copies:
         copy.wait()
 
@@ -391,6 +479,10 @@
             pltpu.VMEM((2, length, head), BF16),
             pltpu.VMEM((BACK_CHUNKS, mp_count) + block, BF16),
             pltpu.VMEM((BACK_CHUNKS, mp_count - 1) + block, BF16),
+            pltpu.VMEM((BACK_CHUNKS, 2) + block, BF16),
+            pltpu.VMEM((BACK_CHUNKS, 2) + block, BF16),
+            pltpu.VMEM((BACK_CHUNKS,) + block, BF16),
+            dma((2,)),
             dma((6,)),
             dma((2,)),
             dma((3, FORWARD_CHUNKS)),

time: 21.1 us -> 21.8 us (1.033)
  Pallas kernels: 20.3 us -> 21 us
    pallas_call x1, Pallas kernels: 19.6 us -> 20.4 us  [shards(): pl.pallas_call(functools.partial(kernel, dp_count, mp_count), out_shape=(...]
where the time goes in v5:
time: 21.8 us; the launch traced here: 21.7 us
  Pallas kernels  21 us (96%)
  between operations  0.64 us (3%)
    pallas_call x1, Pallas kernels, shards(): pl.pallas_call(functools.partial(kernel, dp_count, mp_count), out_shape=(...  20.4 us
    pallas_call x1, Pallas kernels, store(): pl.pallas_call(store_kernel, out_shape=(pltpu.HBM(context.shape, BF16), p...  0.66 us

profile of v5, /device:TPU:0, one launch (start us, length us, event | category | flops | bytes accessed | tf_op | source)
XLA Modules:
  0.0 21.7 jit_solution(1258542763766966923)
XLA Ops:
  0.6 20.4 %shard_map.122 = (bf16[4,16,256]{2,1,0:T(8,128)(2,1)S(1)}, bf16[2,4,4096]{2,1,0:T(4,128)(2,1)S(1)}) custom-call(s32[2]{0:T(128)} %denoiser_hbm.1, s32[2]{0:T(128)} %lengths_hbm.1, s32[2]{0:T(128)} %move_hbm.1, s32[2,16]{1,0:T(2,128)} %span_hbm.1, bf16[3,4096]{1,0:T(4,128)(2,1)} %table_hbm.1, bf16[32,128]{1,0:T(8,128)(2,1)} %bitcast.1, ...), custom_call_target="tpu_custom_call" | custom-call | flops 402653184 | bytes 6815744 | tf_op jit(solution)/shard_map/pallas_call | solution.py:458
  21.0 0.7 %shard_map.123 = (bf16[4,16,256]{2,1,0:T(8,128)(2,1)}, bf16[2,4,4096]{2,1,0:T(4,128)(2,1)}) custom-call(bf16[4,16,256]{2,1,0:T(8,128)(2,1)S(1)} %get-tuple-element.4.context_ref, bf16[2,4,4096]{2,1,0:T(4,128)(2,1)S(1)} %get-tuple-element.5.grad_ref), custom_call_target="tpu_custom_call" | custom-call | tf_op jit(solution)/shard_map/pallas_call | solution.py:425

commit v6 on v4

--- a/solution.py
+++ b/solution.py
@@ -15,8 +15,8 @@
 TN = (((0,), (0,)), ((), ()))
 NN = (((1,), (0,)), ((), ()))
 
-FORWARD_CHUNKS = 4
-BACK_CHUNKS = 8
+FORWARD_CHUNKS = 2
+BACK_CHUNKS = 4
 NORM_CHUNKS = 4
 LANES = 128
 
@@ -132,11 +132,11 @@
         return value
 
     col_row, col_place = split(lax.broadcasted_iota(jnp.int32, (total, 1), 0))
-    lane_row, lane_place = split(lax.broadcasted_iota(jnp.int32, (1, total), 1))
+    lane_row, _ = split(lax.broadcasted_iota(jnp.int32, (1, total), 1))
     natural_lane = lax.broadcasted_iota(jnp.int32, (total, total), 1)
     permute = (natural_lane == col_row * length + col_place).astype(F32).astype(BF16)
     col_len = per_row(col_row, lengths_ref)
-    key_ok = (col_row == lane_row) & (lane_place < jnp.maximum(col_len, 1))
+    key_ok = (col_row == lane_row) & (col_place < jnp.maximum(col_len, 1))
     query_ok = col_place < col_len
 
     def span_column(r, start, count):
@@ -211,12 +211,12 @@
     query = query_f32.astype(BF16)
     key = key_f32.astype(BF16)
     factor = 1.0 / math.sqrt(head)
-    scores = jnp.where(key_ok, matmul(query, key, NT) * factor, -jnp.inf)
+    scores = jnp.where(key_ok, matmul(key, query, NT) * factor, -jnp.inf)
     value_f32 = project(2, 0)
     for chunk in range(1, FORWARD_CHUNKS):
         value_f32 += project(2, chunk)
-    exp_scores = jnp.exp(scores - jnp.max(scores, axis=1, keepdims=True))
-    soft = exp_scores / jnp.sum(exp_scores, axis=1, keepdims=True)
+    exp_scores = jnp.exp(scores - jnp.max(scores, axis=0, keepdims=True))
+    soft = exp_scores / jnp.sum(exp_scores, axis=0, keepdims=True)
     soft_b = soft.astype(BF16)
     value = value_f32.astype(BF16)
     projected = (query_f32, key_f32, value_f32)
@@ -233,12 +233,12 @@
     grad_out = matmul(permute, jnp.concatenate(pieces, axis=0))
     grad_out = jnp.where(query_ok, grad_out, 0.0).astype(BF16)
 
-    grad_value = matmul(soft_b, grad_out, TN).astype(BF16)
-    grad_soft = matmul(grad_out, value, NT)
-    row_inner = jnp.sum(soft * grad_soft, axis=1, keepdims=True)
+    grad_value = matmul(soft_b, grad_out).astype(BF16)
+    grad_soft = matmul(value, grad_out, NT)
+    row_inner = jnp.sum(soft * grad_soft, axis=0, keepdims=True)
     grad_scores = (soft * (grad_soft - row_inner) * factor).astype(BF16)
-    grad_query = matmul(grad_scores, key).astype(BF16)
-    grad_key = matmul(grad_scores, query, TN).astype(BF16)
+    grad_query = matmul(grad_scores, key, TN).astype(BF16)
+    grad_key = matmul(grad_scores, query).astype(BF16)
     gradients = (grad_query, grad_key, grad_value)
     inner = jnp.zeros((total, 1), F32)
     for gradient, result in zip(gradients, projected):
@@ -247,33 +247,48 @@
 
     back_width = width // BACK_CHUNKS
     half = back_width // 2
-    part_copies = []
-    for chunk in range(BACK_CHUNKS):
+
+    def remote(source, target, send_sem, recv_sem, peer):
+        return pltpu.make_async_remote_copy(
+            src_ref=source,
+            dst_ref=target,
+            send_sem=send_sem,
+            recv_sem=recv_sem,
+            device_id={"mp": peer},
+            device_id_type=MESH,
+        )
+
+    def back(chunk):
         piece = pl.ds(chunk * back_width, back_width)
         head_grad = matmul(gradients[0], weights[0, piece, :], NT)
         head_grad += matmul(gradients[1], weights[1, piece, :], NT)
         head_grad += matmul(gradients[2], weights[2, piece, :], NT)
+        return head_grad
+
+    def direct(chunk, step):
+        peer = lax.rem(my_mp + step, mp_count)
+        return remote(
+            part_send.at[chunk, peer],
+            part_recv.at[chunk, step - 1],
+            part_send_sem.at[chunk, step - 1],
+            part_recv_sem.at[chunk, step - 1],
+            peer,
+        )
+
+    head_grad = back(0)
+    for chunk in range(BACK_CHUNKS):
+        piece = pl.ds(chunk * back_width, back_width)
+        following = back(chunk + 1) if chunk + 1 < BACK_CHUNKS else None
         head_part = (head_grad - normed_ref[:, piece] * inner) * inv_rms
         for s in range(mp_count):
             block = head_part[s * seg_total : (s + 1) * seg_total]
             stacked = jnp.concatenate([block[:, :half], block[:, half:]], axis=0)
             part_send[chunk, s] = stacked.astype(BF16)
-        copies = []
         for step in range(1, mp_count):
-            peer = lax.rem(my_mp + step, mp_count)
-            copy = pltpu.make_async_remote_copy(
-                src_ref=part_send.at[chunk, peer],
-                dst_ref=part_recv.at[chunk, step - 1],
-                send_sem=part_send_sem.at[chunk, step - 1],
-                recv_sem=part_recv_sem.at[chunk, step - 1],
-                device_id={"mp": peer},
-                device_id_type=MESH,
-            )
-            copy.start()
-            copies.append(copy)
-        part_copies.append(copies)
-
-    context = jnp.where(query_ok, matmul(soft_b, value), 0.0).astype(BF16)
+            direct(chunk, step).start()
+        head_grad = following
+
+    context = jnp.where(query_ok, matmul(soft_b, value, TN), 0.0).astype(BF16)
     context = matmul(permute, context, TN)
 
     for at, offset in enumerate((1, -1)):
@@ -303,7 +318,7 @@
     for chunk in range(BACK_CHUNKS):
         summed = part_send[chunk, my_mp].astype(F32)
         for step in range(1, mp_count):
-            part_copies[chunk][step - 1].wait_recv()
+            direct(chunk, step).wait_recv()
             summed += part_recv[chunk, step - 1].astype(F32)
         for part in range(2):
             block = jnp.where(
@@ -313,9 +328,9 @@
             for r in range(rows):
                 grad_ref[r, :, columns] = block[r * seg : (r + 1) * seg]
 
-    for copies in part_copies:
-        for copy in copies:
-            copy.wait_send()
+    for chunk in range(BACK_CHUNKS):
+        for step in range(1, mp_count):
+            direct(chunk, step).wait_send()
     for copy in ctx_copies:
         copy.wait()
 

time: 21.1 us -> 20.8 us (0.986)
  Pallas kernels: 20.3 us -> 20 us
    pallas_call x1, Pallas kernels: 19.6 us -> 19.4 us  [shards(): pl.pallas_call(functools.partial(kernel, dp_count, mp_count), out_shape=(...]
where the time goes in v6:
time: 20.8 us; the launch traced here: 20.7 us
  Pallas kernels  20 us (96%)
  between operations  0.64 us (3%)
    pallas_call x1, Pallas kernels, shards(): pl.pallas_call(functools.partial(kernel, dp_count, mp_count), out_shape=(...  19.4 us
    pallas_call x1, Pallas kernels, store(): pl.pallas_call(store_kernel, out_shape=(pltpu.HBM(context.shape, BF16), p...  0.66 us

profile of v6, /device:TPU:0, one launch (start us, length us, event | category | flops | bytes accessed | tf_op | source)
XLA Modules:
  0.0 20.7 jit_solution(13347705774210858444)
XLA Ops:
  0.6 19.4 %shard_map.122 = (bf16[4,16,256]{2,1,0:T(8,128)(2,1)S(1)}, bf16[2,4,4096]{2,1,0:T(4,128)(2,1)S(1)}) custom-call(s32[2]{0:T(128)} %denoiser_hbm.1, s32[2]{0:T(128)} %lengths_hbm.1, s32[2]{0:T(128)} %move_hbm.1, s32[2,16]{1,0:T(2,128)} %span_hbm.1, bf16[3,4096]{1,0:T(4,128)(2,1)} %table_hbm.1, bf16[32,128]{1,0:T(8,128)(2,1)} %bitcast.1, ...), custom_call_target="tpu_custom_call" | custom-call | flops 402653184 | bytes 6815744 | tf_op jit(solution)/shard_map/pallas_call | solution.py:385
  20.0 0.7 %shard_map.123 = (bf16[4,16,256]{2,1,0:T(8,128)(2,1)}, bf16[2,4,4096]{2,1,0:T(4,128)(2,1)}) custom-call(bf16[4,16,256]{2,1,0:T(8,128)(2,1)S(1)} %get-tuple-element.4.context_ref, bf16[2,4,4096]{2,1,0:T(4,128)(2,1)S(1)} %get-tuple-element.5.grad_ref), custom_call_target="tpu_custom_call" | custom-call | tf_op jit(solution)/shard_map/pallas_call | solution.py:352

commit v7 on v6

--- a/solution.py
+++ b/solution.py
@@ -15,7 +15,7 @@
 TN = (((0,), (0,)), ((), ()))
 NN = (((1,), (0,)), ((), ()))
 
-FORWARD_CHUNKS = 2
+FORWARD_CHUNKS = 4
 BACK_CHUNKS = 4
 NORM_CHUNKS = 4
 LANES = 128
@@ -50,8 +50,10 @@
     inputs_ref,
     cot_ref,
     weights,
+    sentinel_row,
     normed_ref,
     normed_b_ref,
+    projected_ref,
     cot_recv,
     ctx_send,
     part_send,
@@ -107,15 +109,18 @@
     load_cot = pltpu.make_async_copy(cot_hbm.at[pl.ds(0, rows)], cot_ref, in_sem.at[1])
     load_cot.start()
     depth = width // FORWARD_CHUNKS
-    loads = []
-    for which, source in enumerate((wq_hbm, wk_hbm, wv_hbm)):
-        for chunk in range(FORWARD_CHUNKS):
-            piece = pl.ds(chunk * depth, depth)
-            load = pltpu.make_async_copy(
+    def load_weights(chunk):
+        piece = pl.ds(pl.multiple_of(chunk * depth, depth), depth)
+        return [
+            pltpu.make_async_copy(
                 source.at[piece], weights.at[which, piece], w_sem.at[which, chunk]
             )
+            for which, source in enumerate((wq_hbm, wk_hbm, wv_hbm))
+        ]
+
+    for chunk in range(FORWARD_CHUNKS):
+        for load in load_weights(chunk):
             load.start()
-            loads.append(load)
 
     for load in small_loads:
         load.wait()
@@ -151,13 +156,14 @@
     denoiser_col = [jnp.full((1, 1), denoiser_ref[r], jnp.int32) for r in range(rows)]
 
     load_inputs.wait()
+    lines = sentinel_ref[...].astype(F32)
+    for line in range(width // LANES):
+        sentinel_row[:, line * LANES : (line + 1) * LANES] = lines[line : line + 1]
     norm_width = width // NORM_CHUNKS
-    squares = jnp.zeros((total, 1), F32)
-    for chunk in range(NORM_CHUNKS):
-        columns = pl.ds(chunk * norm_width, norm_width)
-        lines = norm_width // LANES
-        lines_f32 = sentinel_ref[pl.ds(chunk * lines, lines), :].astype(F32)
-        sentinel = jnp.concatenate([lines_f32[i : i + 1] for i in range(lines)], axis=1)
+
+    def shape_chunk(chunk, squares):
+        columns = pl.ds(pl.multiple_of(chunk * norm_width, norm_width), norm_width)
+        sentinel = sentinel_row[:, columns]
         table = table_ref[:, columns].astype(F32)
         pieces = []
         for r in range(rows):
@@ -168,13 +174,19 @@
             pieces.append(jnp.where(span_natural[r] > 0.5, sentinel, plain).astype(BF16))
         shaped = matmul(permute, jnp.concatenate(pieces, axis=0))
         normed_ref[:, columns] = shaped
-        squares += jnp.sum(shaped * shaped, axis=1, keepdims=True)
+        return squares + jnp.sum(shaped * shaped, axis=1, keepdims=True)
+
+    squares = lax.fori_loop(0, NORM_CHUNKS, shape_chunk, jnp.zeros((total, 1), F32))
     inv_rms = lax.rsqrt(squares * (1.0 / width) + 1e-06)
-    for chunk in range(NORM_CHUNKS):
-        columns = pl.ds(chunk * norm_width, norm_width)
+
+    def norm_chunk(chunk, carry):
+        columns = pl.ds(pl.multiple_of(chunk * norm_width, norm_width), norm_width)
         normed = normed_ref[:, columns] * inv_rms
         normed_ref[:, columns] = normed
         normed_b_ref[:, columns] = normed.astype(BF16)
+        return carry
+
+    lax.fori_loop(0, NORM_CHUNKS, norm_chunk, 0)
 
     pl.semaphore_wait(barrier, 2 + mp_count - 1)
     cot_copies = []
@@ -190,20 +202,19 @@
         copy.start()
         cot_copies.append(copy)
 
-    def project(which, chunk):
-        piece = pl.ds(chunk * depth, depth)
-        return matmul(normed_b_ref[:, piece], weights[which, piece, :])
-
-    query_f32 = jnp.zeros((total, head), F32)
-    key_f32 = jnp.zeros((total, head), F32)
-    for chunk in range(FORWARD_CHUNKS):
-        loads[chunk].wait()
-        query_f32 += project(0, chunk)
-    for chunk in range(FORWARD_CHUNKS):
-        loads[FORWARD_CHUNKS + chunk].wait()
-        key_f32 += project(1, chunk)
-    for chunk in range(FORWARD_CHUNKS):
-        loads[2 * FORWARD_CHUNKS + chunk].wait()
+    projected_ref[...] = jnp.zeros_like(projected_ref)
+
+    def project(chunk, carry):
+        for load in load_weights(chunk):
+            load.wait()
+        piece = pl.ds(pl.multiple_of(chunk * depth, depth), depth)
+        part = normed_b_ref[:, piece]
+        for which in range(3):
+            projected_ref[which] += matmul(part, weights[which, piece, :])
+        return carry
+
+    lax.fori_loop(0, FORWARD_CHUNKS, project, 0)
+    query_f32, key_f32, value_f32 = projected_ref[0], projected_ref[1], projected_ref[2]
     load_cot.wait()
     for copy in cot_copies:
         copy.wait()
@@ -212,9 +223,6 @@
     key = key_f32.astype(BF16)
     factor = 1.0 / math.sqrt(head)
     scores = jnp.where(key_ok, matmul(key, query, NT) * factor, -jnp.inf)
-    value_f32 = project(2, 0)
-    for chunk in range(1, FORWARD_CHUNKS):
-        value_f32 += project(2, chunk)
     exp_scores = jnp.exp(scores - jnp.max(scores, axis=0, keepdims=True))
     soft = exp_scores / jnp.sum(exp_scores, axis=0, keepdims=True)
     soft_b = soft.astype(BF16)
@@ -258,13 +266,6 @@
             device_id_type=MESH,
         )
 
-    def back(chunk):
-        piece = pl.ds(chunk * back_width, back_width)
-        head_grad = matmul(gradients[0], weights[0, piece, :], NT)
-        head_grad += matmul(gradients[1], weights[1, piece, :], NT)
-        head_grad += matmul(gradients[2], weights[2, piece, :], NT)
-        return head_grad
-
     def direct(chunk, step):
         peer = lax.rem(my_mp + step, mp_count)
         return remote(
@@ -275,10 +276,11 @@
             peer,
         )
 
-    head_grad = back(0)
-    for chunk in range(BACK_CHUNKS):
-        piece = pl.ds(chunk * back_width, back_width)
-        following = back(chunk + 1) if chunk + 1 < BACK_CHUNKS else None
+    def back(chunk, carry):
+        piece = pl.ds(pl.multiple_of(chunk * back_width, back_width), back_width)
+        head_grad = matmul(gradients[0], weights[0, piece, :], NT)
+        head_grad += matmul(gradients[1], weights[1, piece, :], NT)
+        head_grad += matmul(gradients[2], weights[2, piece, :], NT)
         head_part = (head_grad - normed_ref[:, piece] * inner) * inv_rms
         for s in range(mp_count):
             block = head_part[s * seg_total : (s + 1) * seg_total]
@@ -286,7 +288,9 @@
             part_send[chunk, s] = stacked.astype(BF16)
         for step in range(1, mp_count):
             direct(chunk, step).start()
-        head_grad = following
+        return carry
+
+    lax.fori_loop(0, BACK_CHUNKS, back, 0)
 
     context = jnp.where(query_ok, matmul(soft_b, value, TN), 0.0).astype(BF16)
     context = matmul(permute, context, TN)
@@ -315,7 +319,7 @@
     span_own = jnp.concatenate(
         [span_column(r, my_mp * seg, seg) for r in range(rows)], axis=0
     )
-    for chunk in range(BACK_CHUNKS):
+    def finish(chunk, carry):
         summed = part_send[chunk, my_mp].astype(F32)
         for step in range(1, mp_count):
             direct(chunk, step).wait_recv()
@@ -324,13 +328,14 @@
             block = jnp.where(
                 span_own > 0.5, 0.0, summed[part * seg_total : (part + 1) * seg_total]
             ).astype(BF16)
-            columns = pl.ds(chunk * back_width + part * half, half)
+            columns = pl.ds(pl.multiple_of(chunk * back_width + part * half, half), half)
             for r in range(rows):
                 grad_ref[r, :, columns] = block[r * seg : (r + 1) * seg]
-
-    for chunk in range(BACK_CHUNKS):
         for step in range(1, mp_count):
             direct(chunk, step).wait_send()
+        return carry
+
+    lax.fori_loop(0, BACK_CHUNKS, finish, 0)
     for copy in ctx_copies:
         copy.wait()
 
@@ -400,8 +405,10 @@
             pltpu.VMEM((rows, length, width), BF16),
             pltpu.VMEM((rows, length, head), BF16),
             pltpu.VMEM((3, width, head), BF16),
+            pltpu.VMEM((1, width), F32),
             pltpu.VMEM((total, width), F32),
             pltpu.VMEM((total, width), BF16),
+            pltpu.VMEM((3, total, head), F32),
             pltpu.VMEM((2, length, head), BF16),
             pltpu.VMEM((2, length, head), BF16),
             pltpu.VMEM((BACK_CHUNKS, mp_count) + block, BF16),

time: 20.8 us -> 21 us (level)
  no operation moved by 1% of the time
where the time goes in v7:
time: 21 us; the launch traced here: 20.9 us
  Pallas kernels  20.2 us (96%)
  between operations  0.64 us (3%)
    pallas_call x1, Pallas kernels, shards(): pl.pallas_call(functools.partial(kernel, dp_count, mp_count), out_shape=(...  19.6 us
    pallas_call x1, Pallas kernels, store(): pl.pallas_call(store_kernel, out_shape=(pltpu.HBM(context.shape, BF16), p...  0.66 us

profile of v7, /device:TPU:0, one launch (start us, length us, event | category | flops | bytes accessed | tf_op | source)
XLA Modules:
  0.0 20.9 jit_solution(18309243695242212406)
XLA Ops:
  0.6 19.6 %shard_map.122 = (bf16[4,16,256]{2,1,0:T(8,128)(2,1)S(1)}, bf16[2,4,4096]{2,1,0:T(4,128)(2,1)S(1)}) custom-call(s32[2]{0:T(128)} %denoiser_hbm.1, s32[2]{0:T(128)} %lengths_hbm.1, s32[2]{0:T(128)} %move_hbm.1, s32[2,16]{1,0:T(2,128)} %span_hbm.1, bf16[3,4096]{1,0:T(4,128)(2,1)} %table_hbm.1, bf16[32,128]{1,0:T(8,128)(2,1)} %bitcast.1, ...), custom_call_target="tpu_custom_call" | custom-call | flops 402653184 | bytes 6815744 | tf_op jit(solution)/shard_map/pallas_call | solution.py:390
  20.2 0.7 %shard_map.123 = (bf16[4,16,256]{2,1,0:T(8,128)(2,1)}, bf16[2,4,4096]{2,1,0:T(4,128)(2,1)}) custom-call(bf16[4,16,256]{2,1,0:T(8,128)(2,1)S(1)} %get-tuple-element.4.context_ref, bf16[2,4,4096]{2,1,0:T(4,128)(2,1)S(1)} %get-tuple-element.5.grad_ref), custom_call_target="tpu_custom_call" | custom-call | tf_op jit(solution)/shard_map/pallas_call | solution.py:357

commit v8 on v6

--- a/solution.py
+++ b/solution.py
@@ -258,12 +258,12 @@
             device_id_type=MESH,
         )
 
+    joined = jnp.concatenate(gradients, axis=1)
+
     def back(chunk):
         piece = pl.ds(chunk * back_width, back_width)
-        head_grad = matmul(gradients[0], weights[0, piece, :], NT)
-        head_grad += matmul(gradients[1], weights[1, piece, :], NT)
-        head_grad += matmul(gradients[2], weights[2, piece, :], NT)
-        return head_grad
+        beside = jnp.concatenate([weights[which, piece, :] for which in range(3)], axis=1)
+        return matmul(beside, joined, NT).T
 
     def direct(chunk, step):
         peer = lax.rem(my_mp + step, mp_count)

time: 20.8 us -> 20.9 us (level)
  no operation moved by 1% of the time
where the time goes in v8:
time: 20.9 us; the launch traced here: 20.7 us
  Pallas kernels  20.1 us (96%)
  between operations  0.64 us (3%)
    pallas_call x1, Pallas kernels, shards(): pl.pallas_call(functools.partial(kernel, dp_count, mp_count), out_shape=(...  19.4 us
    pallas_call x1, Pallas kernels, store(): pl.pallas_call(store_kernel, out_shape=(pltpu.HBM(context.shape, BF16), p...  0.66 us

profile of v8, /device:TPU:0, one launch (start us, length us, event | category | flops | bytes accessed | tf_op | source)
XLA Modules:
  0.0 20.7 jit_solution(8852153011853867606)
XLA Ops:
  0.6 19.4 %shard_map.122 = (bf16[4,16,256]{2,1,0:T(8,128)(2,1)S(1)}, bf16[2,4,4096]{2,1,0:T(4,128)(2,1)S(1)}) custom-call(s32[2]{0:T(128)} %denoiser_hbm.1, s32[2]{0:T(128)} %lengths_hbm.1, s32[2]{0:T(128)} %move_hbm.1, s32[2,16]{1,0:T(2,128)} %span_hbm.1, bf16[3,4096]{1,0:T(4,128)(2,1)} %table_hbm.1, bf16[32,128]{1,0:T(8,128)(2,1)} %bitcast.1, ...), custom_call_target="tpu_custom_call" | custom-call | flops 402653184 | bytes 6815744 | tf_op jit(solution)/shard_map/pallas_call | solution.py:385
  20.0 0.7 %shard_map.123 = (bf16[4,16,256]{2,1,0:T(8,128)(2,1)}, bf16[2,4,4096]{2,1,0:T(4,128)(2,1)}) custom-call(bf16[4,16,256]{2,1,0:T(8,128)(2,1)S(1)} %get-tuple-element.4.context_ref, bf16[2,4,4096]{2,1,0:T(4,128)(2,1)S(1)} %get-tuple-element.5.grad_ref), custom_call_target="tpu_custom_call" | custom-call | tf_op jit(solution)/shard_map/pallas_call | solution.py:352

commit v9 on v5

--- a/solution.py
+++ b/solution.py
@@ -321,12 +321,6 @@
                 direct(chunk, step).start()
         head_grad = following
 
-    if paired:
-        mate_copy = remote(
-            part_send.at[:, mate], mate_recv, mate_sem.at[0], mate_sem.at[1], mate
-        )
-        mate_copy.start()
-
     context = jnp.where(query_ok, matmul(soft_b, value), 0.0).astype(BF16)
     context = matmul(permute, context, TN)
 
@@ -351,7 +345,24 @@
         own = jnp.where(moves(r, 0), context[r * length : (r + 1) * length], 0.0)
         context_ref[r] = own.astype(BF16)
 
+    def own_pair(chunk):
+        return remote(
+            part_send.at[chunk, mate],
+            mate_recv.at[chunk],
+            mate_sem.at[0, chunk],
+            mate_sem.at[1, chunk],
+            mate,
+        )
+
     if paired:
+
+        @pl.when(outer)
+        def _():
+            for chunk in range(BACK_CHUNKS):
+                to_mate(chunk).wait_send()
+
+        for chunk in range(BACK_CHUNKS):
+            own_pair(chunk).start()
 
         @pl.when(jnp.logical_not(outer))
         def _():
@@ -363,7 +374,6 @@
                     pair_send[chunk, j] = partial.astype(BF16)
                     from_inner(chunk, j).start()
 
-        mate_copy.wait_recv()
 
     span_own = jnp.concatenate(
         [span_column(r, my_mp * seg, seg) for r in range(rows)], axis=0
@@ -371,6 +381,7 @@
     for chunk in range(BACK_CHUNKS):
         summed = part_send[chunk, my_mp].astype(F32)
         if paired:
+            own_pair(chunk).wait_recv()
             summed += mate_recv[chunk].astype(F32)
             from_inner(chunk, 0).wait_recv()
             summed += part_recv[chunk, 0].astype(F32)
@@ -387,12 +398,8 @@
                 grad_ref[r, :, columns] = block[r * seg : (r + 1) * seg]
 
     if paired:
-        mate_copy.wait_send()
-
-        @pl.when(outer)
-        def _():
-            for chunk in range(BACK_CHUNKS):
-                to_mate(chunk).wait_send()
+        for chunk in range(BACK_CHUNKS):
+            own_pair(chunk).wait_send()
 
         @pl.when(jnp.logical_not(outer))
         def _():
@@ -482,7 +489,7 @@
             pltpu.VMEM((BACK_CHUNKS, 2) + block, BF16),
             pltpu.VMEM((BACK_CHUNKS, 2) + block, BF16),
             pltpu.VMEM((BACK_CHUNKS,) + block, BF16),
-            dma((2,)),
+            dma((2, BACK_CHUNKS)),
             dma((6,)),
             dma((2,)),
             dma((3, FORWARD_CHUNKS)),

time: 21.8 us -> 21.5 us (0.986)
  Pallas kernels: 21 us -> 20.7 us
    pallas_call x1, Pallas kernels: 20.4 us -> 20 us  [shards(): pl.pallas_call(functools.partial(kernel, dp_count, mp_count), out_shape=(...]
where the time goes in v9:
time: 21.5 us; the launch traced here: 21.3 us
  Pallas kernels  20.7 us (96%)
  between operations  0.64 us (3%)
    pallas_call x1, Pallas kernels, shards(): pl.pallas_call(functools.partial(kernel, dp_count, mp_count), out_shape=(...  20 us
    pallas_call x1, Pallas kernels, store(): pl.pallas_call(store_kernel, out_shape=(pltpu.HBM(context.shape, BF16), p...  0.66 us

profile of v9, /device:TPU:0, one launch (start us, length us, event | category | flops | bytes accessed | tf_op | source)
XLA Modules:
  0.0 21.3 jit_solution(9607289631409112617)
XLA Ops:
  0.6 20.0 %shard_map.122 = (bf16[4,16,256]{2,1,0:T(8,128)(2,1)S(1)}, bf16[2,4,4096]{2,1,0:T(4,128)(2,1)S(1)}) custom-call(s32[2]{0:T(128)} %denoiser_hbm.1, s32[2]{0:T(128)} %lengths_hbm.1, s32[2]{0:T(128)} %move_hbm.1, s32[2,16]{1,0:T(2,128)} %span_hbm.1, bf16[3,4096]{1,0:T(4,128)(2,1)} %table_hbm.1, bf16[32,128]{1,0:T(8,128)(2,1)} %bitcast.1, ...), custom_call_target="tpu_custom_call" | custom-call | flops 402653184 | bytes 6815744 | tf_op jit(solution)/shard_map/pallas_call | solution.py:465
  20.6 0.7 %shard_map.123 = (bf16[4,16,256]{2,1,0:T(8,128)(2,1)}, bf16[2,4,4096]{2,1,0:T(4,128)(2,1)}) custom-call(bf16[4,16,256]{2,1,0:T(8,128)(2,1)S(1)} %get-tuple-element.4.context_ref, bf16[2,4,4096]{2,1,0:T(4,128)(2,1)S(1)} %get-tuple-element.5.grad_ref), custom_call_target="tpu_custom_call" | custom-call | tf_op jit(solution)/shard_map/pallas_call | solution.py:432
